TPU v7x, 1024 devices: a whole 4x4x32 slice. The times are simulated.
1024 devices in a mesh: row: 8 (over x, core), col: 128 (over y, z).
Axes of the slice: x: 4, y: 4, z: 32, core: 2. Of those that a mesh axis runs over, the one named last changes fastest.
Arguments:
- fields: float32 [1024, 4, 32, 1024], P(('row', 'col')), may hold values from -6 to 6
- fluid_mask: int32 [1024, 32, 1024], P(('row', 'col')), may hold values 0 or 1
- body_force: float32 [3], replicated, may hold values from -3 to 3
- neighbours: int32 [1024, 6], P(('row', 'col')), may hold values from -1 to 0, as said below
- sources: int32 [1024, 8], P(('row', 'col')), may hold values from -1 to 127, as said below
Outputs:
- new_fields: float32 [1024, 4, 32, 1024], P(('row', 'col'))
- coarse_residual: float32 [1024, 512], P(('row', 'col'))
Inputs may be any that keep to these rules, and one draw needn't show every extreme that they name: `neighbours`: entries 0 and 1 name a slot on the device one lower or higher along row, 2 and 3 along col, 4 and 5 on the own device; links are mutual. `sources`: every fine tile of a row group is named exactly once among that row group's entries; one device's entries name at most 4 tiles, and some device reaches that in every draw.
All inputs are finite; a program needn't handle non-finite values. No bound on the sum of `fluid_mask` on one device may be relied on, other than what follows from the above.
Results may differ from a plain program's by a relative error of at most 0.00002.
Values sent between devices are 32-bit elements; how exact they have to be, the bound alone decides.
A program may use at most 32 MiB of HBM per device.

v0:
```python
import jax
import jax.numpy as jnp
from jax import lax
from jax.sharding import PartitionSpec as P

TILE = 32
SWEEPS = 2


RELAXATION = 0.8
PRESSURE_RATE = 0.5


def extended(cells, sides, width):
    for axis, dim in sides:
        count = lax.axis_size(axis)
        ends = count - 1
        head = lax.slice_in_dim(cells, 0, width, axis=dim)
        tail = lax.slice_in_dim(cells, cells.shape[dim] - width, cells.shape[dim], axis=dim)
        cells = jnp.concatenate(
            [
                lax.ppermute(tail, axis, [(i, (i + 1) % count) for i in range(ends)]),
                cells,
                lax.ppermute(head, axis, [((i + 1) % count, i) for i in range(ends)]),
            ],
            axis=dim,
        )
    return cells


def tile_faces(values, edge_cells):
    low_x = values[:, :, 0, :]
    high_x = values[:, :, -1, :]
    low_y = values[..., :edge_cells]
    high_y = values[..., -edge_cells:]
    low_z = values[..., ::edge_cells]
    high_z = values[..., edge_cells - 1 :: edge_cells]
    return (low_x, high_x, low_y, high_y, low_z, high_z)


def neighbour_values(values, planes, edge_cells):
    minus_x, plus_x, minus_y, plus_y, minus_z, plus_z = planes
    below_x = jnp.concatenate([minus_x[:, :, None, :], values[:, :, :-1, :]], axis=2)
    above_x = jnp.concatenate([values[:, :, 1:, :], plus_x[:, :, None, :]], axis=2)
    below_y = jnp.concatenate([minus_y, values[..., :-edge_cells]], axis=3)
    above_y = jnp.concatenate([values[..., edge_cells:], plus_y], axis=3)
    depth_index = jnp.arange(edge_cells * edge_cells, dtype=jnp.int32) % edge_cells
    zero_col = jnp.zeros(values.shape[:3] + (1,), values.dtype)
    below_z = jnp.where(
        depth_index == 0,
        jnp.repeat(minus_z, edge_cells, axis=3),
        jnp.concatenate([zero_col, values[..., :-1]], axis=3),
    )
    above_z = jnp.where(
        depth_index == edge_cells - 1,
        jnp.repeat(plus_z, edge_cells, axis=3),
        jnp.concatenate([values[..., 1:], zero_col], axis=3),
    )
    return (below_x, above_x, below_y, above_y, below_z, above_z)


def velocity_step(fields, planes, fluid, body_force, edge_cells):
    velocity = fields[:, :3]
    pressure = fields[:, 3:]
    below_x, above_x, below_y, above_y, below_z, above_z = neighbour_values(
        fields, planes, edge_cells
    )
    beside_all = below_x + above_x + (below_y + above_y) + (below_z + above_z)
    laplace = beside_all[:, :3] - 6.0 * velocity
    gradient = jnp.concatenate(
        [pressure - below_x[:, 3:], pressure - below_y[:, 3:], pressure - below_z[:, 3:]], axis=1
    )
    momentum_residual = body_force[None, :, None, None] + laplace - gradient
    return velocity + RELAXATION / 6.0 * fluid[:, None] * momentum_residual


def pressure_step(velocity, pressure, above, fluid, edge_cells):
    plus_x, plus_y, plus_z = above
    along_x = velocity[:, 0]
    along_y = velocity[:, 1]
    along_z = velocity[:, 2]
    next_x = jnp.concatenate([along_x[:, 1:, :], plus_x[:, None, :]], axis=1)
    next_y = jnp.concatenate([along_y[..., edge_cells:], plus_y], axis=2)
    depth_index = jnp.arange(edge_cells * edge_cells, dtype=jnp.int32) % edge_cells
    zero_col = jnp.zeros(along_z.shape[:2] + (1,), along_z.dtype)
    next_z = jnp.where(
        depth_index == edge_cells - 1,
        jnp.repeat(plus_z, edge_cells, axis=2),
        jnp.concatenate([along_z[..., 1:], zero_col], axis=2),
    )
    residual = fluid * (next_x - along_x + (next_y - along_y) + (next_z - along_z))
    return (pressure + PRESSURE_RATE * residual[:, None], residual)


def restrict(residual, edge_cells):
    tile_count = residual.shape[0]
    block_edge = edge_cells // 4
    coarse_grid = residual.reshape(tile_count, 4, block_edge, 4, block_edge, 4, block_edge)
    return jnp.sum(coarse_grid, axis=(2, 4, 6)).reshape(tile_count, 64) / float(
        block_edge * block_edge
    )


def assemble(octants):
    coarse_count = octants.shape[0]
    coarse_grid = octants.reshape(coarse_count, 2, 2, 2, 4, 4, 4)
    return coarse_grid.transpose(0, 1, 4, 2, 5, 3, 6).reshape(coarse_count, 512)


def select_slots(slot_ids, source):
    source_count = source.shape[0]
    matches = slot_ids[:, None] == jnp.arange(source_count, dtype=jnp.int32)[None, :]
    matches = matches.reshape(matches.shape + (1,) * (source.ndim - 1))
    return jnp.sum(jnp.where(matches, source[None], jnp.zeros((), source.dtype)), axis=1)


def full_planes(fields, neighbours, edge_cells):
    low_x, high_x, low_y, high_y, low_z, high_z = tile_faces(fields, edge_cells)
    tile_count = fields.shape[0]
    field_count = fields.shape[1]
    rows_ext = extended(jnp.stack([low_x, high_x]), (("row", 0),), 1)
    flat_y = jnp.stack([low_y, high_y]).reshape(2, tile_count, field_count, edge_cells * edge_cells)
    cols_ext = extended(flat_y, (("col", 0),), 1)
    minus_x = select_slots(neighbours[:, 0], rows_ext[0])
    plus_x = select_slots(neighbours[:, 1], rows_ext[3])
    minus_y = select_slots(neighbours[:, 2], cols_ext[0]).reshape(
        tile_count, field_count, edge_cells, edge_cells
    )
    plus_y = select_slots(neighbours[:, 3], cols_ext[3]).reshape(
        tile_count, field_count, edge_cells, edge_cells
    )
    minus_z = select_slots(neighbours[:, 4], high_z)
    plus_z = select_slots(neighbours[:, 5], low_z)
    return (minus_x, plus_x, minus_y, plus_y, minus_z, plus_z)


def on_device(fields, fluid_mask, body_force, neighbours, sources):
    edge_cells = TILE
    fluid = fluid_mask.astype(jnp.float32)
    residual = None
    for sweep_index in range(SWEEPS):
        planes = full_planes(fields, neighbours, edge_cells)
        velocity = velocity_step(fields, planes, fluid, body_force, edge_cells)
        refreshed = full_planes(
            jnp.concatenate([velocity, fields[:, 3:]], axis=1), neighbours, edge_cells
        )
        above = (refreshed[1][:, 0], refreshed[3][:, 1], refreshed[5][:, 2])
        pressure, residual = pressure_step(velocity, fields[:, 3:], above, fluid, edge_cells)
        fields = jnp.concatenate([velocity, pressure], axis=1)
    restricted = restrict(residual, edge_cells)
    shard_rows = lax.all_gather(restricted, "col", axis=0, tiled=True)
    positions = jnp.arange(shard_rows.shape[0], dtype=jnp.int32)
    matches = sources[:, :, None] == positions[None, None, :]
    octants = jnp.sum(
        jnp.where(matches[..., None], shard_rows[None, None], jnp.zeros((), shard_rows.dtype)),
        axis=2,
    )
    return (fields, assemble(octants))


def solution(mesh):
    return jax.shard_map(
        on_device,
        mesh=mesh,
        in_specs=(
            P(("row", "col"), None, None, None),
            P(("row", "col"), None, None),
            P(),
            P(("row", "col"), None),
            P(("row", "col"), None),
        ),
        out_specs=(P(("row", "col"), None, None, None), P(("row", "col"), None)),
        check_vma=False,
    )
```

profile of v0, /device:TPU:4, one launch (start us, length us, event | category | flops | bytes accessed | tf_op | source)
XLA Modules:
  0.0 263.1 jit_solution(17032780754084628855)
XLA Ops:
  1.8 3.8 %collective-permute-start.2 = (f32[1,1,4,1024]{3,0,2,1:T(1,128)S(1)}, f32[1,1,4,1024]{3,0,2,1:T(1,128)S(1)}, u32[]{:S(2)}, u32[]{:S(2)}) collective-permute-start(f32[1,1,4,1024]{3,0,2,1:T(1,128)S(1)} %slice.245), channel_id=1, source_target_pairs={{0,1},{1,2},{2,3},{3,4},{4,5},{5,6},{6,7},{7,8},{8,9},{9,10},{10,1... | collective-permute-start | bytes 49160 | tf_op jit(solution)/shard_map/ppermute | solution.py:22
  6.6 1.9 collective-permute-start
  9.9 3.6 %collective-permute-start.1 = (f32[1,1,4,1024]{3,0,2,1:T(1,128)S(1)}, f32[1,1,4,1024]{3,0,2,1:T(1,128)S(1)}, u32[]{:S(2)}, u32[]{:S(2)}) collective-permute-start(f32[1,1,4,1024]{3,0,2,1:T(1,128)S(1)} %get-tuple-element.24), channel_id=1, source_target_pairs={{128,0},{256,128},{384,256},{512,384},{640,512},{768,640},{896,768... | collective-permute-start | bytes 49160 | tf_op jit(solution)/shard_map/ppermute | solution.py:24
  15.2 2.3 fusion.58
  22.3 1.7 broadcast_in_dim.212
  25.3 1.7 broadcast_in_dim.217
  37.2 1.7 fusion.12
  39.5 1.7 slice.271
  43.3 2.1 collective-permute-start.4
  45.6 2.1 collective-permute-done.5
  48.8 1.7 slice.285
  50.5 2.1 fusion.53
  54.2 2.1 fusion.51
  61.9 4.5 %collective-permute-start.8 = (f32[1,1,4,1024]{3,0,2,1:T(1,128)S(1)}, f32[1,1,4,1024]{3,0,2,1:T(1,128)S(1)}, u32[]{:S(2)}, u32[]{:S(2)}) collective-permute-start(f32[1,1,4,1024]{3,0,2,1:T(1,128)S(1)} %slice.306), channel_id=1, source_target_pairs={{0,1},{1,2},{2,3},{3,4},{4,5},{5,6},{6,7},{7,8},{8,9},{9,10},{10,1... | collective-permute-start | bytes 49160 | tf_op jit(solution)/shard_map/ppermute | solution.py:22
  66.4 3.3 %collective-permute-start.7 = (f32[1,1,4,1024]{3,0,2,1:T(1,128)}, f32[1,1,4,1024]{3,0,2,1:T(1,128)}, u32[]{:S(2)}, u32[]{:S(2)}) collective-permute-start(f32[1,1,4,1024]{3,0,2,1:T(1,128)} %get-tuple-element.10), channel_id=1, source_target_pairs={{128,0},{256,128},{384,256},{512,384},{640,512},{768,640},{896,768... | collective-permute-start | bytes 49160 | tf_op jit(solution)/shard_map/ppermute | solution.py:24
  69.7 2.2 broadcast_select_fusion.1
  73.4 1.7 broadcast_in_dim.224
  75.2 2.1 collective-permute-start.6
  77.5 8.9 %collective-permute-done.6 = f32[1,1,4,1024]{3,0,2,1:T(1,128)S(1)} collective-permute-done((f32[1,1,4,1024]{3,0,2,1:T(1,128)S(1)}, f32[1,1,4,1024]{3,0,2,1:T(1,128)S(1)}, u32[]{:S(2)}, u32[]{:S(2)}) %collective-permute-start.6) | collective-permute-done | bytes 16416 | tf_op jit(solution)/shard_map/ppermute | solution.py:22
  88.0 3.8 %fusion.16 = f32[1,3,32,1024]{3,0,2,1:T(1,128)S(1)} fusion(pred[1024]{0:T(1024)(128)(4,1)} %copy-done.21, f32[1,4,32,1024]{3,0,2,1:T(1,128)S(1)} %copy-done.11, f32[1,4,32,1023]{3,0,2,1:T(1,128)S(1)} %copy-done.6, f32[1,4,32,1024]{3,0,2,1:T(1,128)} %broadcast_in_dim.224, f32[1,4,1,1024]{3,0,2,1:T(1,128)S(1)} %fusion.37, ...), kind=kLoop, calls=%fused_computation.29 | loop fusion | flops 983040 | bytes 3801600 | tf_op jit(solution)/shard_map/add | solution.py:68
  92.7 1.7 slice.302
  96.7 3.4 %collective-permute-start.10 = (f32[1,1,4,1024]{3,0,2,1:T(1,128)S(1)}, f32[1,1,4,1024]{3,0,2,1:T(1,128)S(1)}, u32[]{:S(2)}, u32[]{:S(2)}) collective-permute-start(f32[1,1,4,1024]{3,0,2,1:T(1,128)S(1)} %slice_bitcast_fusion.7), channel_id=1, source_target_pairs={{128,0},{256,128},{384,256},{512,384},{640,512},{768,640},{896,768... | collective-permute-start | bytes 49160 | tf_op jit(solution)/shard_map/ppermute | solution.py:24
  101.6 2.5 reshape.663
  104.7 156.4 %all-gather = f32[128,1,64]{2,1,0:T(1,128)S(1)} all-gather(f32[1,1,64]{2,1,0:T(1,128)S(1)} %reshape.666), channel_id=1, replica_groups=mesh['row'=8,'col'=128] {'col'}, dimensions={0}, use_global_device_ids=true | all-gather | bytes 33024 | tf_op jit(solution)/shard_map/all_gather | solution.py:151
  (170 shorter events, 38.7 us)
Async XLA Ops:
  0.6 16.9 %copy-start = (f32[1,4,32,1024]{3,2,1,0:T(8,128)S(1)}, f32[1,4,32,1024]{3,2,1,0:T(8,128)}, u32[]{:S(2)}) copy-start(f32[1,4,32,1024]{3,2,1,0:T(8,128)} %param.5) | copy-start | bytes 1572868
  1.8 33.6 %collective-permute-start.2 = (f32[1,1,4,1024]{3,0,2,1:T(1,128)S(1)}, f32[1,1,4,1024]{3,0,2,1:T(1,128)S(1)}, u32[]{:S(2)}, u32[]{:S(2)}) collective-permute-start(f32[1,1,4,1024]{3,0,2,1:T(1,128)S(1)} %slice.245), channel_id=1, source_target_pairs={{0,1},{1,2},{2,3},{3,4},{4,5},{5,6},{6,7},{7,8},{8,9},{9,10},{10,1... | collective-permute-start | bytes 49160 | tf_op jit(solution)/shard_map/ppermute | solution.py:22
  6.6 28.9 %collective-permute-start = (f32[1,1,4,1024]{3,0,2,1:T(1,128)S(1)}, f32[1,1,4,1024]{3,0,2,1:T(1,128)S(1)}, u32[]{:S(2)}, u32[]{:S(2)}) collective-permute-start(f32[1,1,4,1024]{3,0,2,1:T(1,128)S(1)} %get-tuple-element.25), channel_id=1, source_target_pairs={{0,128},{128,256},{256,384},{384,512},{512,640},{640,768},{768,896... | collective-permute-start | bytes 49160 | tf_op jit(solution)/shard_map/ppermute | solution.py:22
  8.6 27.7 %collective-permute-start.3 = (f32[1,1,4,1024]{3,0,2,1:T(1,128)S(1)}, f32[1,1,4,1024]{3,0,2,1:T(1,128)S(1)}, u32[]{:S(2)}, u32[]{:S(2)}) collective-permute-start(f32[1,1,4,1024]{3,0,2,1:T(1,128)S(1)} %slice.250), channel_id=1, source_target_pairs={{1,0},{2,1},{3,2},{4,3},{5,4},{6,5},{7,6},{8,7},{9,8},{10,9},{11,1... | collective-permute-start | bytes 49160 | tf_op jit(solution)/shard_map/ppermute | solution.py:24
  9.9 27.2 %collective-permute-start.1 = (f32[1,1,4,1024]{3,0,2,1:T(1,128)S(1)}, f32[1,1,4,1024]{3,0,2,1:T(1,128)S(1)}, u32[]{:S(2)}, u32[]{:S(2)}) collective-permute-start(f32[1,1,4,1024]{3,0,2,1:T(1,128)S(1)} %get-tuple-element.24), channel_id=1, source_target_pairs={{128,0},{256,128},{384,256},{512,384},{640,512},{768,640},{896,768... | collective-permute-start | bytes 49160 | tf_op jit(solution)/shard_map/ppermute | solution.py:24
  17.6 11.8 %copy-start.24 = (pred[1024]{0:T(1024)(128)(4,1)}, pred[1024]{0:T(1024)(128)(4,1)S(1)}, u32[]{:S(2)}) copy-start(pred[1024]{0:T(1024)(128)(4,1)S(1)} %fusion.48) | copy-start | bytes 3076
  20.3 10.6 %copy-start.21 = (pred[1024]{0:T(1024)(128)(4,1)}, pred[1024]{0:T(1024)(128)(4,1)S(1)}, u32[]{:S(2)}) copy-start(pred[1024]{0:T(1024)(128)(4,1)S(1)} %fusion.47) | copy-start | bytes 3076
  41.5 6.2 %collective-permute-start.5 = (f32[1,1,4,1024]{3,0,2,1:T(1,128)S(1)}, f32[1,1,4,1024]{3,0,2,1:T(1,128)S(1)}, u32[]{:S(2)}, u32[]{:S(2)}) collective-permute-start(f32[1,1,4,1024]{3,0,2,1:T(1,128)S(1)} %slice.269), channel_id=1, source_target_pairs={{1,0},{2,1},{3,2},{4,3},{5,4},{6,5},{7,6},{8,7},{9,8},{10,9},{11,1... | collective-permute-start | bytes 49160 | tf_op jit(solution)/shard_map/ppermute | solution.py:24
  43.3 4.6 %collective-permute-start.4 = (f32[1,1,4,1024]{3,0,2,1:T(1,128)S(1)}, f32[1,1,4,1024]{3,0,2,1:T(1,128)S(1)}, u32[]{:S(2)}, u32[]{:S(2)}) collective-permute-start(f32[1,1,4,1024]{3,0,2,1:T(1,128)S(1)} %slice_bitcast_fusion.11), channel_id=1, source_target_pairs={{128,0},{256,128},{384,256},{512,384},{640,512},{768,640},{896,768... | collective-permute-start | bytes 49160 | tf_op jit(solution)/shard_map/ppermute | solution.py:24
  58.8 10.9 %copy-start.25 = (pred[1024]{0:T(1024)(128)(4,1)S(1)}, pred[1024]{0:T(1024)(128)(4,1)}, u32[]{:S(2)}) copy-start(pred[1024]{0:T(1024)(128)(4,1)} %copy-done.24) | copy-start | bytes 3076
  59.4 12.5 %copy-start.2 = (f32[1,1,32,1024]{3,2,1,0:T(8,128)S(1)}, f32[1,1,32,1024]{3,2,1,0:T(8,128)}, u32[]{:S(2)}) copy-start(f32[1,1,32,1024]{3,2,1,0:T(8,128)} %copy-done.1) | copy-start | bytes 393220
  60.5 27.2 %collective-permute-start.9 = (f32[1,1,4,1024]{3,0,2,1:T(1,128)S(1)}, f32[1,1,4,1024]{3,0,2,1:T(1,128)S(1)}, u32[]{:S(2)}, u32[]{:S(2)}) collective-permute-start(f32[1,1,4,1024]{3,0,2,1:T(1,128)S(1)} %slice.284), channel_id=1, source_target_pairs={{1,0},{2,1},{3,2},{4,3},{5,4},{6,5},{7,6},{8,7},{9,8},{10,9},{11,1... | collective-permute-start | bytes 49160 | tf_op jit(solution)/shard_map/ppermute | solution.py:24
  61.9 15.4 %collective-permute-start.8 = (f32[1,1,4,1024]{3,0,2,1:T(1,128)S(1)}, f32[1,1,4,1024]{3,0,2,1:T(1,128)S(1)}, u32[]{:S(2)}, u32[]{:S(2)}) collective-permute-start(f32[1,1,4,1024]{3,0,2,1:T(1,128)S(1)} %slice.306), channel_id=1, source_target_pairs={{0,1},{1,2},{2,3},{3,4},{4,5},{5,6},{6,7},{7,8},{8,9},{9,10},{10,1... | collective-permute-start | bytes 49160 | tf_op jit(solution)/shard_map/ppermute | solution.py:22
  66.4 21.5 %collective-permute-start.7 = (f32[1,1,4,1024]{3,0,2,1:T(1,128)}, f32[1,1,4,1024]{3,0,2,1:T(1,128)}, u32[]{:S(2)}, u32[]{:S(2)}) collective-permute-start(f32[1,1,4,1024]{3,0,2,1:T(1,128)} %get-tuple-element.10), channel_id=1, source_target_pairs={{128,0},{256,128},{384,256},{512,384},{640,512},{768,640},{896,768... | collective-permute-start | bytes 49160 | tf_op jit(solution)/shard_map/ppermute | solution.py:24
  72.8 13.5 %copy-start.3 = (f32[1,4,32,992]{3,0,2,1:T(1,128)S(1)}, f32[1,4,32,992]{3,0,2,1:T(1,128)}, u32[]{:S(2)}) copy-start(f32[1,4,32,992]{3,0,2,1:T(1,128)} %get-tuple-element.7) | copy-start | bytes 1523716
  75.2 12.8 %copy-start.5 = (f32[1,4,31,1024]{3,0,2,1:T(1,128)S(1)}, f32[1,4,31,1024]{3,0,2,1:T(1,128)}, u32[]{:S(2)}) copy-start(f32[1,4,31,1024]{3,0,2,1:T(1,128)} %get-tuple-element.9) | copy-start | bytes 1523716
  75.2 12.8 %copy-start.6 = (f32[1,4,32,1023]{3,0,2,1:T(1,128)S(1)}, f32[1,4,32,1023]{3,0,2,1:T(1,128)}, u32[]{:S(2)}) copy-start(f32[1,4,32,1023]{3,0,2,1:T(1,128)} %get-tuple-element.12) | copy-start | bytes 1571332
  75.2 12.8 %copy-start.7 = (f32[1,4,32,992]{3,0,2,1:T(1,128)S(1)}, f32[1,4,32,992]{3,0,2,1:T(1,128)}, u32[]{:S(2)}) copy-start(f32[1,4,32,992]{3,0,2,1:T(1,128)} %get-tuple-element.6) | copy-start | bytes 1523716
  75.2 12.9 %copy-start.11 = (f32[1,4,32,1024]{3,0,2,1:T(1,128)S(1)}, f32[1,4,32,1024]{3,0,2,1:T(1,128)}, u32[]{:S(2)}) copy-start(f32[1,4,32,1024]{3,0,2,1:T(1,128)} %copy-done.10) | copy-start | bytes 1572868
  75.2 11.1 %collective-permute-start.6 = (f32[1,1,4,1024]{3,0,2,1:T(1,128)S(1)}, f32[1,1,4,1024]{3,0,2,1:T(1,128)S(1)}, u32[]{:S(2)}, u32[]{:S(2)}) collective-permute-start(f32[1,1,4,1024]{3,0,2,1:T(1,128)S(1)} %get-tuple-element.11), channel_id=1, source_target_pairs={{0,128},{128,256},{256,384},{384,512},{512,640},{640,768},{768,896... | collective-permute-start | bytes 49160 | tf_op jit(solution)/shard_map/ppermute | solution.py:22
  92.1 9.4 %copy-start.15 = (s32[1,32,1024]{2,1,0:T(8,128)S(1)}, s32[1,32,1024]{2,1,0:T(8,128)}, u32[]{:S(2)}) copy-start(s32[1,32,1024]{2,1,0:T(8,128)} %param.6) | copy-start | bytes 393220
  94.7 6.4 %collective-permute-start.11 = (f32[1,1,4,1024]{3,0,2,1:T(1,128)S(1)}, f32[1,1,4,1024]{3,0,2,1:T(1,128)S(1)}, u32[]{:S(2)}, u32[]{:S(2)}) collective-permute-start(f32[1,1,4,1024]{3,0,2,1:T(1,128)S(1)} %slice.300), channel_id=1, source_target_pairs={{1,0},{2,1},{3,2},{4,3},{5,4},{6,5},{7,6},{8,7},{9,8},{10,9},{11,1... | collective-permute-start | bytes 49160 | tf_op jit(solution)/shard_map/ppermute | solution.py:24
  96.7 4.8 %collective-permute-start.10 = (f32[1,1,4,1024]{3,0,2,1:T(1,128)S(1)}, f32[1,1,4,1024]{3,0,2,1:T(1,128)S(1)}, u32[]{:S(2)}, u32[]{:S(2)}) collective-permute-start(f32[1,1,4,1024]{3,0,2,1:T(1,128)S(1)} %slice_bitcast_fusion.7), channel_id=1, source_target_pairs={{128,0},{256,128},{384,256},{512,384},{640,512},{768,640},{896,768... | collective-permute-start | bytes 49160 | tf_op jit(solution)/shard_map/ppermute | solution.py:24
  101.6 159.6 %copy-start.27 = (pred[8,128]{1,0:T(8,128)(4,1)S(1)}, pred[8,128]{1,0:T(8,128)(4,1)}, u32[]{:S(2)}) copy-start(pred[8,128]{1,0:T(8,128)(4,1)} %iota_compare_fusion) | copy-start | bytes 3076
  (17 other events, 76.9 us)
where the time goes:
time: 264 us; the launch traced here: 263 us
  blocking collectives  156 us (59%)
  local copies, waits for them, and re-layouts  42.6 us (16%)
  starting transfers between devices  30.1 us (11%)
  other arithmetic  16.5 us (6%)
  waiting for transfers between devices  12 us (5%)
  between operations  5.42 us (2%)
    all_gather x1, blocking collectives, on_device(): shard_rows = lax.all_gather(restricted, 'col', axis=0, tiled=True)  156 us
    ppermute x8, starting transfers between devices, extended(): lax.ppermute(head, axis, [((i + 1) % count, i) for i in range(ends)])  17.8 us
    ppermute x4, starting transfers between devices, extended(): lax.ppermute(tail, axis, [(i, (i + 1) % count) for i in range(ends)])  12.3 us
    ppermute x4, waiting for transfers between devices, extended(): lax.ppermute(tail, axis, [(i, (i + 1) % count) for i in range(ends)])  8.87 us
    slice x4, local copies, waits for them, and re-layouts, tile_faces(): low_z = values[..., ::edge_cells]  5.55 us
  transfers between devices with their start and end apart: 12, of which 4 were waited for; matrix products, arithmetic and copies ran while one was open for 11% of the time, Pallas kernels for 0%

commit v1 on v0

v1 whole, which is shorter than its diff:
```python
import functools

import jax
import jax.numpy as jnp
from jax import lax
from jax.experimental import pallas as pl
from jax.experimental.pallas import tpu as pltpu
from jax.sharding import PartitionSpec as P

MESH = pl.DeviceIdType.MESH
TILE = 32
RATE = 0.8 / 6.0
PRESSURE_RATE = 0.5
OFF = 8
PLANES = 48
NEAR = 5
FAR = 11
SLOTS = 33


def roll(values, shift, axis):
    return pltpu.roll(values, shift % values.shape[axis], axis)


def kernel(
    rows, y_count, z_count,
    neighbour_ref, source_ref, force_ref, fields_ref, mask_ref, fields_out, coarse_out,
    ext, mask_raw, vel1, pres1, vel2, pres2, halo0, halo1, halo2, gate_x, gate_lo, gate_hi,
    send_lo, send_hi, recv_lo, recv_hi, table, row_buf,
    load_sem, store_sem, send_sem, recv_sem, gsend_sem, grecv_sem, know_sem,
):
    f32 = jnp.float32
    cols = y_count * z_count
    r = lax.axis_index("row")
    c = lax.axis_index("col")
    y, z = c // z_count, lax.rem(c, z_count)

    def tile_at(dr, dc):
        return (lax.rem(r + dr + rows, rows), lax.rem(c + dc + cols, cols))

    def along(dy, dz):
        return (r, lax.rem(y + dy, y_count) * z_count + lax.rem(z + dz + z_count, z_count))

    greeted = [tile_at(dr, dc) for dr in (-1, 0, 1) for dc in (-1, 0, 1) if (dr, dc) != (0, 0)]
    greeted += [along(0, -1), along(0, 1)] + [along(j, 0) for j in range(1, y_count)]
    barrier = pltpu.get_barrier_semaphore()
    for device in greeted:
        pl.semaphore_signal(barrier, inc=1, device_id=device, device_id_type=MESH)

    loads = []
    for s in range(8):
        lanes = pl.ds(128 * s, 128)
        loads.append(pltpu.make_async_copy(fields_ref.at[:, :, lanes], ext.at[pl.ds(0, 4), pl.ds(OFF, TILE), s], load_sem.at[s]))
        loads.append(pltpu.make_async_copy(mask_ref.at[:, lanes], mask_raw.at[:, s], load_sem.at[8 + s]))
    for copy in loads:
        copy.start()

    sub = lax.broadcasted_iota(jnp.int32, (8, 128), 0)
    lane = lax.broadcasted_iota(jnp.int32, (8, 128), 1)
    depth = lane % TILE
    lane_long = lax.broadcasted_iota(jnp.int32, (PLANES, 128), 1)
    zero = jnp.zeros((8, 128), f32)
    one = jnp.ones((8, 128), f32)

    def link(direction, exists):
        return jnp.where(jnp.logical_and(neighbour_ref[0, direction] == 0, exists), 1.0, 0.0).astype(f32)

    links = [link(0, r > 0), link(1, r < rows - 1), link(2, c > 0), link(3, c < cols - 1), link(4, True), link(5, True)]
    own = zero
    for d in range(6):
        own = jnp.where(sub == d, links[d], own)

    for x in (0, 1, 2, 30, 31):
        ext[5, OFF + x] = own

    def flag(tile, d):
        return jnp.broadcast_to(tile[d : d + 1, :], (8, 128))

    own_z_lo = jnp.where(depth == 0, flag(own, 4), one)
    own_z_hi = jnp.where(depth == TILE - 1, flag(own, 5), one)
    gate_x[...] = jnp.ones((PLANES, 8, 128), f32)
    gate_x[OFF] = flag(own, 0)
    gate_x[OFF + TILE] = flag(own, 1)
    gate_lo[pl.ds(OFF, TILE)] = jnp.broadcast_to(own_z_lo[None], (TILE, 8, 128))
    gate_hi[pl.ds(OFF, TILE)] = jnp.broadcast_to(own_z_hi[None], (TILE, 8, 128))

    for copy in loads:
        copy.wait()
    ext[4, pl.ds(OFF, TILE)] = mask_raw[...].astype(f32)

    lane_tile = lax.broadcasted_iota(jnp.int32, (TILE, 128), 1)
    flags_tile = jnp.concatenate([own] * 4, axis=0)
    top = [ext[f, pl.ds(OFF, TILE), 7, :] for f in range(5)]
    send_hi[0] = jnp.where(lane_tile >= 64, top[0], roll(top[1], 64, 1))
    send_hi[1] = jnp.where(lane_tile >= 64, top[2], roll(top[3], 64, 1))
    send_hi[2] = jnp.where(lane_tile >= 64, top[4], flags_tile)
    low = [ext[f, pl.ds(OFF, TILE), 0, :] for f in range(5)]
    send_lo[0] = jnp.where(lane_tile < 96, low[0], flags_tile)
    send_lo[1] = low[1]
    send_lo[2] = low[2]
    send_lo[3] = jnp.where(lane_tile < 64, low[3], roll(low[4], 64, 1))

    pl.semaphore_wait(barrier, len(greeted))

    whole, first, last = pl.ds(OFF, TILE), pl.ds(0, 8), pl.ds(24, 8)
    below, above = pl.ds(0, 8), pl.ds(OFF + TILE, 8)
    plan = [
        (send_hi, recv_lo, slice(None), whole, (0, 1)),
        (send_lo, recv_hi, slice(None), whole, (0, -1)),
        (send_hi, recv_lo, last, below, (1, 1)),
        (send_hi, recv_lo, first, above, (-1, 1)),
        (send_lo, recv_hi, last, below, (1, -1)),
        (send_lo, recv_hi, first, above, (-1, -1)),
    ]
    faces = []
    for k, (src, dst, src_rows, dst_rows, offset) in enumerate(plan):
        faces.append(pltpu.make_async_remote_copy(
            src_ref=src if k < 2 else src.at[:, src_rows], dst_ref=dst.at[:, dst_rows], send_sem=send_sem.at[k], recv_sem=recv_sem.at[k],
            device_id=tile_at(*offset), device_id_type=MESH))
    faces.append(pltpu.make_async_remote_copy(
        src_ref=ext.at[:, pl.ds(OFF + 30, 2)], dst_ref=ext.at[:, pl.ds(OFF - 2, 2)], send_sem=send_sem.at[6], recv_sem=recv_sem.at[6],
        device_id=tile_at(1, 0), device_id_type=MESH))
    faces.append(pltpu.make_async_remote_copy(
        src_ref=ext.at[:, pl.ds(OFF, 3)], dst_ref=ext.at[:, pl.ds(OFF + TILE, 3)], send_sem=send_sem.at[7], recv_sem=recv_sem.at[7],
        device_id=tile_at(-1, 0), device_id_type=MESH))
    for copy in faces:
        copy.start()

    def tell(step, reach):
        for device in (along(0, reach), along(0, -reach)):
            pl.semaphore_signal(know_sem.at[step], inc=1, device_id=device, device_id_type=MESH)

    def hear(step):
        pl.semaphore_wait(know_sem.at[step], 2)

    tell(0, 1)
    hear(0)
    tell(1, 2)

    for copy in faces:
        copy.wait()

    row_lo, row_hi = ext[5, OFF - 1], ext[5, OFF + TILE]

    def spread_lo(tile):
        return jnp.where(lane < 64, tile, roll(tile, 64, 1))

    def spread_hi(tile):
        half = jnp.where(lane >= 96, tile, roll(tile, 96, 1))
        return jnp.where(lane >= 64, half, roll(half, 64, 1))

    col_lo = [spread_lo(recv_lo[2, k : k + 8]) for k in (0, OFF, OFF + TILE)]
    col_hi = [spread_hi(recv_hi[0, k : k + 8]) for k in (0, OFF, OFF + TILE)]
    mid = [row_lo, own, row_hi]
    for k, x, n in ((0, OFF - 2, 2), (2, OFF + TILE, 3)):
        gate_lo[pl.ds(x, n)] = jnp.broadcast_to(jnp.where(depth == 0, flag(mid[k], 4), one)[None], (n, 8, 128))
        gate_hi[pl.ds(x, n)] = jnp.broadcast_to(jnp.where(depth == TILE - 1, flag(mid[k], 5), one)[None], (n, 8, 128))

    def by_region(tiles):
        return jnp.concatenate([tiles[0]] + [tiles[1]] * 4 + [tiles[2]], axis=0)

    def strip_gates(outer, is_own, crossing, d):
        z_lo, z_hi, cross = [], [], []
        for k in range(3):
            z_lo.append(jnp.where(depth == 0, jnp.where(is_own, flag(mid[k], 4), flag(outer[k], 4)), one))
            z_hi.append(jnp.where(depth == TILE - 1, jnp.where(is_own, flag(mid[k], 5), flag(outer[k], 5)), one))
            cross.append(jnp.where(crossing, flag(mid[k], d), one))
        x_lo = jnp.where(sub == 0, jnp.where(is_own, flag(own, 0), flag(outer[1], 0)), one)
        x_hi = jnp.where(sub == 0, jnp.where(is_own, flag(own, 1), flag(outer[1], 1)), one)
        x_gate = jnp.concatenate([one, x_lo, one, one, one, x_hi], axis=0)
        return x_gate, by_region(cross), by_region(z_lo), by_region(z_hi)

    lo_gates = strip_gates(col_lo, lane >= 64, lane // TILE == 2, 2)
    hi_gates = strip_gates(col_hi, lane < 32, lane // TILE == 1, 3)
    cross_lo = by_region([flag(tile, 2) for tile in mid])
    cross_hi = by_region([flag(tile, 3) for tile in mid])

    raw = [recv_lo[0], recv_lo[1], recv_lo[2]]
    outer = [roll(raw[0], 64, 1), raw[0], roll(raw[1], 64, 1), raw[1], roll(raw[2], 64, 1)]
    lo = [jnp.where(lane_long < 64, outer[f], roll(ext[f, :, 0, :], 64, 1)) for f in range(5)]
    raw = [recv_hi[k] for k in range(4)]
    outer = [roll(raw[0], 32, 1), roll(raw[1], 32, 1), roll(raw[2], 32, 1), roll(raw[3], 32, 1), roll(raw[3], 96, 1)]
    hi = [jnp.where(lane_long < 32, roll(ext[f, :, 7, :], 32, 1), outer[f]) for f in range(5)]

    depth_long = lane_long % TILE

    def strip_below(v, gates):
        x_gate, y_gate, z_lo, _ = gates
        return (
            roll(v, 1, 0) * x_gate,
            roll(v, 32, 1) * y_gate,
            jnp.where(depth_long == 0, roll(v, -31, 1), roll(v, 1, 1)) * z_lo,
        )

    def strip_above(v, gates):
        x_gate, y_gate, _, z_hi = gates
        return (
            roll(v * x_gate, -1, 0),
            roll(v * y_gate, -32, 1),
            jnp.where(depth_long == TILE - 1, roll(v, 31, 1), roll(v, -1, 1)) * z_hi,
        )

    def strip_velocity(v, p, m, gates, wanted):
        under = strip_below(p, gates)
        result = []
        for d in wanted:
            b, a = strip_below(v[d], gates), strip_above(v[d], gates)
            laplace = (b[0] + a[0]) + (b[1] + a[1]) + (b[2] + a[2]) - 6.0 * v[d]
            result.append(v[d] + RATE * m * (force_ref[d] + laplace - (p - under[d])))
        return result

    def strip_pressure(v, p, m, gates):
        total = zero_strip
        for d in range(3):
            total = total + (strip_above(v[d], gates)[d] - v[d])
        return p + PRESSURE_RATE * (m * total)

    zero_strip = jnp.zeros((PLANES, 128), f32)

    def put_lo(dst, v):
        dst[:, 0, :] = roll(v, 64, 1) * cross_lo

    def put_hi(dst, v):
        dst[:, 7, :] = roll(v, 96, 1) * cross_hi

    for f in range(4):
        put_lo(halo0.at[f], lo[f])
        if f < 3:
            put_hi(halo0.at[f], hi[f])
    lo1 = strip_velocity(lo[:3], lo[3], lo[4], lo_gates, (0, 1, 2))
    hi1 = strip_velocity(hi[:3], hi[3], hi[4], hi_gates, (0, 1, 2))
    for d in range(3):
        put_lo(halo1.at[d], lo1[d])
        put_hi(halo1.at[d], hi1[d])
    lo_p1 = strip_pressure(lo1, lo[3], lo[4], lo_gates)
    hi_p1 = strip_pressure(hi1, hi[3], hi[4], hi_gates)
    put_lo(halo1.at[3], lo_p1)

    def below_y(v, h):
        w = jnp.where(sub3 == 0, h, roll(v, 1, 1))
        return roll(jnp.where(lane3 >= 96, w, v), 32, 2)

    def above_y(v, h):
        w = jnp.where(sub3 == 7, h, roll(v, -1, 1))
        return roll(jnp.where(lane3 < 32, w, v), -32, 2)

    def below_z(v, g):
        return jnp.where(lane3 % TILE == 0, roll(v, -31, 2), roll(v, 1, 2)) * g

    def above_z(v, g):
        return jnp.where(lane3 % TILE == TILE - 1, roll(v, 31, 2), roll(v, -1, 2)) * g

    def planes(x, n):
        return pl.ds(OFF + x, n)

    def velocity_planes(x, n, v_in, p_in, halo, v_out):
        here, under, over = planes(x, n), planes(x - 1, n), planes(x + 1, n)
        g_under, g_over, g_lo, g_hi = gate_x[here], gate_x[over], gate_lo[here], gate_hi[here]
        scale = RATE * ext[4, here]
        p = p_in[here]
        p_below = (p_in[under] * g_under, below_y(p, halo[3, here]), below_z(p, g_lo))
        for d in range(3):
            v, h = v_in[d, here], halo[d, here]
            total = (v_in[d, under] * g_under + v_in[d, over] * g_over) + (below_y(v, h) + above_y(v, h))
            total = total + (below_z(v, g_lo) + above_z(v, g_hi)) - 6.0 * v
            v_out[d, here] = v + scale * (force_ref[d] + total - (p - p_below[d]))

    def divergence_planes(x, n, v_in, halo_y):
        here, over = planes(x, n), planes(x + 1, n)
        vx, vy, vz = v_in[0, here], v_in[1, here], v_in[2, here]
        total = (v_in[0, over] * gate_x[over] - vx) + (above_y(vy, halo_y[here]) - vy) + (above_z(vz, gate_hi[here]) - vz)
        return ext[4, here] * total

    step = 5
    shape3 = (step, 8, 128)
    sub3 = lax.broadcasted_iota(jnp.int32, shape3, 1)
    lane3 = lax.broadcasted_iota(jnp.int32, shape3, 2)
    for x in range(-1, 34, step):
        velocity_planes(x, step, ext, ext.at[3], halo0, vel1)

    hear(1)
    tell(2, 4)
    tell(3, 1)

    for x in range(-1, 32, step):
        pres1[planes(x, step)] = ext[3, planes(x, step)] + PRESSURE_RATE * divergence_planes(x, step, vel1, halo1.at[1])

    hi1 = [jnp.where(lane_long < 32, roll(vel1[d, :, 7, :], 32, 1), hi1[d]) for d in range(3)]
    hi_p1 = jnp.where(lane_long < 32, roll(pres1[:, 7, :], 32, 1), hi_p1)
    put_hi(halo2, strip_velocity(hi1, hi_p1, hi[4], hi_gates, (1,))[0])

    step = 3
    shape3 = (step, 8, 128)
    sub3 = lax.broadcasted_iota(jnp.int32, shape3, 1)
    lane3 = lax.broadcasted_iota(jnp.int32, shape3, 2)
    for x in range(0, 33, step):
        velocity_planes(x, step, vel1, pres1, halo1, vel2)

    step = 8
    shape3 = (step, 8, 128)
    sub3 = lax.broadcasted_iota(jnp.int32, shape3, 1)
    lane3 = lax.broadcasted_iota(jnp.int32, shape3, 2)
    message = zero
    for x in range(0, TILE, step):
        div = divergence_planes(x, step, vel2, halo2)
        pres2[pl.ds(x, step)] = pres1[planes(x, step)] + PRESSURE_RATE * div
        part = jnp.sum(div, axis=0)
        for shift in (1, 2, 4):
            part = part + jnp.where((lane // shift) % 2 == 0, roll(part, -shift, 1), roll(part, shift, 1))
        part = part + roll(part, 32, 1)
        part = part + roll(part, 64, 1)
        part = part + jnp.where(sub % 2 == 0, roll(part, -1, 0), roll(part, 1, 0))
        message = jnp.where(jnp.logical_and(lane // 32 == x // 8, sub == 2 * ((lane % 8) // 2)), part, message)
    table[0, z_count // 2] = jnp.sum(message, axis=0, keepdims=True) * (1.0 / 64.0)

    hear(3)
    middle = z_count // 2
    near = []
    for k in range(1, NEAR + 1):
        for sign in (1, -1):
            index = len(near)
            near.append(pltpu.make_async_remote_copy(
                src_ref=table.at[0, middle], dst_ref=table.at[0, middle - sign * k], send_sem=gsend_sem.at[index], recv_sem=grecv_sem.at[index],
                device_id=along(0, sign * k), device_id_type=MESH))
    for copy in reversed(near):
        copy.start()

    stores = []
    for s in range(8):
        lanes = pl.ds(128 * s, 128)
        stores.append(pltpu.make_async_copy(vel2.at[:, pl.ds(OFF, TILE), s], fields_out.at[pl.ds(0, 3), :, lanes], store_sem.at[s]))
        stores.append(pltpu.make_async_copy(pres2.at[:, s], fields_out.at[3, :, lanes], store_sem.at[8 + s]))
    for copy in stores:
        copy.start()

    hear(2)
    tell(4, 3)

    for copy in near:
        copy.wait()
    hear(4)
    block = pl.ds(middle - NEAR, 2 * NEAR + 1)
    far = []
    for k, sign in enumerate((1, -1)):
        landed = pl.ds(middle - NEAR - sign * FAR, 2 * NEAR + 1)
        index = len(near) + k
        far.append(pltpu.make_async_remote_copy(
            src_ref=table.at[0, block], dst_ref=table.at[0, landed], send_sem=gsend_sem.at[index], recv_sem=grecv_sem.at[index],
            device_id=along(0, sign * FAR), device_id_type=MESH))
    for copy in far:
        copy.start()
    for copy in far:
        copy.wait()
    across = []
    for j in range(1, y_count):
        index = len(near) + len(far) + j - 1
        across.append(pltpu.make_async_remote_copy(
            src_ref=table.at[0], dst_ref=table.at[y_count - j], send_sem=gsend_sem.at[index], recv_sem=grecv_sem.at[index],
            device_id=along(j, 0), device_id_type=MESH))
    for copy in across:
        copy.start()

    spot = lax.broadcasted_iota(jnp.int32, (128, 512), 1)
    entry = (spot // 64) % 4 * 32 + spot % 4 * 8 + (spot // 8) % 4 * 2
    pick = jnp.where(lax.broadcasted_iota(jnp.int32, (128, 512), 0) == entry, 1.0, 0.0).astype(f32)
    spot = lax.broadcasted_iota(jnp.int32, (8, 512), 1)
    octant = spot // 256 * 4 + (spot // 32) % 2 * 2 + (spot // 4) % 2
    holds = lax.broadcasted_iota(jnp.int32, (8, 512), 0) == octant

    for copy in across:
        copy.wait()
    for o in range(8):
        source = source_ref[0, o]
        kept = jnp.maximum(source, 0)
        dy = lax.rem(kept // z_count - y + y_count, y_count)
        dz = lax.rem(lax.rem(kept, z_count) - z + z_count + middle, z_count)
        taken = table[dy, dz]
        row_buf[pl.ds(o, 1), :] = jnp.where(source >= 0, taken, jnp.zeros_like(taken))
    spread = jnp.dot(row_buf[...], pick, preferred_element_type=f32, precision=lax.Precision.HIGHEST)
    coarse_out[...] = jnp.sum(jnp.where(holds, spread, 0.0), axis=0, keepdims=True)

    for copy in stores:
        copy.wait()


def on_device(rows, fields, fluid_mask, body_force, neighbours, sources):
    y_count, z_count = 4, 32
    f32 = jnp.float32
    volume = lambda n: pltpu.VMEM((n, PLANES, 8, 128), f32)
    planes = lambda: pltpu.VMEM((PLANES, 8, 128), f32)
    near = 2 * NEAR + 2 + y_count - 1
    any_space = pl.BlockSpec(memory_space=pl.ANY)
    scalars = pl.BlockSpec(memory_space=pltpu.SMEM)
    new_fields, coarse = pl.pallas_call(
        functools.partial(kernel, rows, y_count, z_count),
        out_shape=(
            jax.ShapeDtypeStruct((4, TILE, TILE * TILE), f32),
            jax.ShapeDtypeStruct((1, 512), f32),
        ),
        in_specs=[scalars, scalars, scalars, any_space, any_space],
        out_specs=(any_space, pl.BlockSpec(memory_space=pltpu.VMEM)),
        scratch_shapes=[
            volume(6),
            pltpu.VMEM((TILE, 8, 128), jnp.int32),
            volume(3),
            planes(),
            volume(3),
            pltpu.VMEM((TILE, 8, 128), f32),
            volume(4),
            volume(4),
            planes(),
            planes(),
            planes(),
            planes(),
            pltpu.VMEM((4, TILE, 128), f32),
            pltpu.VMEM((3, TILE, 128), f32),
            pltpu.VMEM((3, PLANES, 128), f32),
            pltpu.VMEM((4, PLANES, 128), f32),
            pltpu.VMEM((y_count, SLOTS, 1, 128), f32),
            pltpu.VMEM((8, 128), f32),
            pltpu.SemaphoreType.DMA((16,)),
            pltpu.SemaphoreType.DMA((16,)),
            pltpu.SemaphoreType.DMA((8,)),
            pltpu.SemaphoreType.DMA((8,)),
            pltpu.SemaphoreType.DMA((near,)),
            pltpu.SemaphoreType.DMA((near,)),
            pltpu.SemaphoreType.REGULAR((5,)),
        ],
        compiler_params=pltpu.CompilerParams(
            collective_id=0, has_side_effects=True, vmem_limit_bytes=60 * 1024 * 1024
        ),
    )(
        neighbours,
        sources,
        body_force,
        fields.reshape(4, TILE, TILE * TILE),
        fluid_mask.reshape(TILE, TILE * TILE),
    )
    return new_fields[None], coarse


def solution(mesh):
    return jax.shard_map(
        functools.partial(on_device, mesh.shape["row"]),
        mesh=mesh,
        in_specs=(
            P(("row", "col"), None, None, None),
            P(("row", "col"), None, None),
            P(),
            P(("row", "col"), None),
            P(("row", "col"), None),
        ),
        out_specs=(P(("row", "col"), None, None, None), P(("row", "col"), None)),
        check_vma=False,
    )
```

time: 264 us -> 52.1 us (0.20)
  the two profiles are of different devices: /device:TPU:4 before, /device:TPU:2 now
where the time goes in v1:
time: 52.1 us; the launch traced here: 51.8 us
  Pallas kernels  48.7 us (93%)
  local copies, waits for them, and re-layouts  2.47 us (5%)
  between operations  0.65 us (1%)
    pallas_call x1, Pallas kernels, on_device(): pl.pallas_call(functools.partial(kernel, rows, y_count, z_count), out_sha...  48.7 us
    unnamed x4, local copies, waits for them, and re-layouts  2.47 us

profile of v1, /device:TPU:2, one launch (start us, length us, event | category | flops | bytes accessed | tf_op | source)
XLA Modules:
  0.0 51.8 jit_solution(13271357603047873298)
XLA Ops:
  0.6 48.7 %shard_map.68 = (f32[4,32,1024]{2,1,0:T(8,128)}, f32[1,512]{1,0:T(1,128)}) custom-call(s32[1,6]{1,0:T(1,128)} %neighbour_ref.1, s32[1,8]{1,0:T(1,128)} %source_ref.1, f32[3]{0:T(128)} %force_ref.1, f32[4,32,1024]{2,1,0:T(8,128)} %bitcast.3, s32[32,1024]{1,0:T(8,128)} %bitcast.5), custom_call_target="tpu_custom_call" | custom-call | tf_op jit(solution)/shard_map/pallas_call | solution.py:394
  49.3 0.0 copy-start
  49.3 1.9 %copy.9 = f32[1,4,32,1024]{3,2,1,0:T(8,128)} copy(f32[1,4,32,1024]{3,2,1,0:T(8,128)} %bitcast.4) | data formatting | bytes 1048576
  51.2 0.0 copy-done
  51.2 0.6 %copy.10 = f32[1,512]{1,0:T(1,128)} copy(f32[1,512]{1,0:T(1,128)S(1)} %copy-done) | data formatting | bytes 4096
Async XLA Ops:
  49.3 1.9 %copy-start = (f32[1,512]{1,0:T(1,128)S(1)}, f32[1,512]{1,0:T(1,128)}, u32[]{:S(2)}) copy-start(f32[1,512]{1,0:T(1,128)} %get-tuple-element.9) | copy-start | bytes 6148

commit v2 on v1

v2 whole, which is shorter than its diff:
```python
import functools

import jax
import jax.numpy as jnp
from jax import lax
from jax.experimental import pallas as pl
from jax.experimental.pallas import tpu as pltpu
from jax.sharding import PartitionSpec as P

MESH = pl.DeviceIdType.MESH
TILE = 32
RATE = 0.8 / 6.0
PRESSURE_RATE = 0.5
OFF = 8
PLANES = 48
NEAR = 5
FAR = 11
SLOTS = 33
GATHER_COPIES = 2 * NEAR + 2 + 9


def roll(values, shift, axis):
    return pltpu.roll(values, shift % values.shape[axis], axis)


def kernel(
    rows, y_count, z_count,
    neighbour_hbm, source_hbm, force_hbm, fields_ref, mask_ref, fields_out, coarse_out,
    neighbour_ref, source_ref, force_ref,
    ext, mask_raw, vel1, pres1, vel2, pres2, halo1, halo2, gate_x, gate_lo, gate_hi,
    send_lo, send_hi, recv_lo, recv_hi, send_corner, recv_corner, table, row_buf,
    load_sem, store_sem, send_sem, recv_sem, gsend_sem, grecv_sem, know_sem,
):
    f32 = jnp.float32
    cols = y_count * z_count
    r = lax.axis_index("row")
    c = lax.axis_index("col")
    y, z = c // z_count, lax.rem(c, z_count)

    def tile_at(dr, dc):
        return (lax.rem(r + dr + rows, rows), lax.rem(c + dc + cols, cols))

    def along(dy, dz):
        return (r, lax.rem(y + dy, y_count) * z_count + lax.rem(z + dz + z_count, z_count))

    greeted = [tile_at(dr, dc) for dr in (-1, 1) for dc in (-1, 1)]
    greeted += [tile_at(0, -1), tile_at(0, 1), tile_at(-1, 0), tile_at(1, 0)]
    greeted += [along(0, -1), along(0, 1), along(1, 0), along(y_count - 1, 0)]
    barrier = pltpu.get_barrier_semaphore()
    for device in greeted:
        pl.semaphore_signal(barrier, inc=1, device_id=device, device_id_type=MESH)

    smalls = [
        pltpu.make_async_copy(neighbour_hbm, neighbour_ref, load_sem.at[16]),
        pltpu.make_async_copy(source_hbm, source_ref, load_sem.at[17]),
        pltpu.make_async_copy(force_hbm, force_ref, load_sem.at[18]),
    ]
    for copy in smalls:
        copy.start()

    loads = []
    for s in range(8):
        lanes = pl.ds(128 * s, 128)
        loads.append(pltpu.make_async_copy(fields_ref.at[:, :, lanes], ext.at[pl.ds(0, 4), pl.ds(OFF, TILE), s], load_sem.at[s]))
        loads.append(pltpu.make_async_copy(mask_ref.at[:, lanes], mask_raw.at[:, s], load_sem.at[8 + s]))
    for copy in loads:
        copy.start()

    sub = lax.broadcasted_iota(jnp.int32, (8, 128), 0)
    lane = lax.broadcasted_iota(jnp.int32, (8, 128), 1)
    depth = lane % TILE
    lane_long = lax.broadcasted_iota(jnp.int32, (PLANES, 128), 1)
    zero = jnp.zeros((8, 128), f32)
    one = jnp.ones((8, 128), f32)

    for copy in smalls:
        copy.wait()

    def link(direction, exists):
        return jnp.where(jnp.logical_and(neighbour_ref[0, direction] == 0, exists), 1.0, 0.0).astype(f32)

    links = [link(0, r > 0), link(1, r < rows - 1), link(2, c > 0), link(3, c < cols - 1), link(4, True), link(5, True)]
    own = zero
    for d in range(6):
        own = jnp.where(sub == d, links[d], own)

    for x in (0, 1, 2, 30, 31):
        ext[5, OFF + x] = own

    def flag(tile, d):
        return jnp.broadcast_to(tile[d : d + 1, :], (8, 128))

    own_z_lo = jnp.where(depth == 0, flag(own, 4), one)
    own_z_hi = jnp.where(depth == TILE - 1, flag(own, 5), one)
    gate_x[...] = jnp.ones((PLANES, 8, 128), f32)
    gate_x[OFF] = flag(own, 0)
    gate_x[OFF + TILE] = flag(own, 1)
    gate_lo[pl.ds(OFF, TILE)] = jnp.broadcast_to(own_z_lo[None], (TILE, 8, 128))
    gate_hi[pl.ds(OFF, TILE)] = jnp.broadcast_to(own_z_hi[None], (TILE, 8, 128))

    for copy in loads:
        copy.wait()
    ext[4, pl.ds(OFF, TILE)] = mask_raw[...].astype(f32)

    lane_tile = lax.broadcasted_iota(jnp.int32, (TILE, 128), 1)
    flags_tile = jnp.concatenate([own] * 4, axis=0)
    top = [ext[f, pl.ds(OFF, TILE), 7, :] for f in range(5)]
    send_hi[0] = jnp.where(lane_tile >= 64, top[0], roll(top[1], 64, 1))
    send_hi[1] = jnp.where(lane_tile >= 64, top[2], roll(top[3], 64, 1))
    send_hi[2] = jnp.where(lane_tile >= 64, top[4], flags_tile)
    low = [ext[f, pl.ds(OFF, TILE), 0, :] for f in range(5)]
    send_lo[0] = jnp.where(lane_tile < 64, low[0], roll(low[2], 64, 1))
    send_lo[1] = jnp.where(lane_tile < 96, low[1], flags_tile)
    send_lo[2] = jnp.where(lane_tile < 64, low[3], roll(low[4], 64, 1))

    def corner(packed, x, up):
        tile = jnp.where(sub == 6, flag(own, 4), flag(own, 5))
        for g in range(3):
            tile = jnp.where(sub // 2 == g, roll(packed[g, x : x + 8], 2 * g - up, 0), tile)
        return tile

    send_corner[0] = corner(send_hi, 24, 6)
    send_corner[1] = corner(send_hi, 0, 0)
    send_corner[2] = corner(send_lo, 24, 6)
    send_corner[3] = corner(send_lo, 0, 0)

    pl.semaphore_wait(barrier, len(greeted))

    plan = [(send_corner.at[k], recv_corner.at[k], offset) for k, offset in enumerate([(1, 1), (-1, 1), (1, -1), (-1, -1)])]
    plan += [(send_hi, recv_lo, (0, 1)), (send_lo, recv_hi, (0, -1))]
    faces = []
    for k, (src, dst, offset) in enumerate(plan):
        faces.append(pltpu.make_async_remote_copy(
            src_ref=src, dst_ref=dst, send_sem=send_sem.at[k], recv_sem=recv_sem.at[k], device_id=tile_at(*offset), device_id_type=MESH))
    faces.append(pltpu.make_async_remote_copy(
        src_ref=ext.at[:, pl.ds(OFF + 30, 2)], dst_ref=ext.at[:, pl.ds(OFF - 2, 2)], send_sem=send_sem.at[6], recv_sem=recv_sem.at[6],
        device_id=tile_at(1, 0), device_id_type=MESH))
    faces.append(pltpu.make_async_remote_copy(
        src_ref=ext.at[:, pl.ds(OFF, 3)], dst_ref=ext.at[:, pl.ds(OFF + TILE, 3)], send_sem=send_sem.at[7], recv_sem=recv_sem.at[7],
        device_id=tile_at(-1, 0), device_id_type=MESH))
    for copy in faces:
        copy.start()

    def tell(step, reach):
        for device in (along(0, reach), along(0, -reach)):
            pl.semaphore_signal(know_sem.at[step], inc=1, device_id=device, device_id_type=MESH)

    def hear(step):
        pl.semaphore_wait(know_sem.at[step], 2)

    tell(0, 1)
    for j in (1, y_count - 1):
        pl.semaphore_signal(know_sem.at[5], inc=1, device_id=along(j, 0), device_id_type=MESH)

    def iotas(shape):
        return lax.broadcasted_iota(jnp.int32, shape, 1), lax.broadcasted_iota(jnp.int32, shape, 2)

    def below_y(v, h):
        w = jnp.where(sub3 == 0, 0.0 if h is None else h, roll(v, 1, 1))
        return roll(jnp.where(lane3 >= 96, w, v), 32, 2)

    def above_y(v, h):
        w = jnp.where(sub3 == 7, 0.0 if h is None else h, roll(v, -1, 1))
        return roll(jnp.where(lane3 < 32, w, v), -32, 2)

    def below_z(v, g):
        return jnp.where(lane3 % TILE == 0, roll(v, -31, 2), roll(v, 1, 2)) * g

    def above_z(v, g):
        return jnp.where(lane3 % TILE == TILE - 1, roll(v, 31, 2), roll(v, -1, 2)) * g

    def planes(x, n):
        return pl.ds(OFF + x, n)

    def velocity_planes(x, n, v_in, p_in, halo, v_out):
        here, under, over = planes(x, n), planes(x - 1, n), planes(x + 1, n)
        g_under, g_over, g_lo, g_hi = gate_x[here], gate_x[over], gate_lo[here], gate_hi[here]
        scale = RATE * ext[4, here]
        p = p_in[here]
        p_below = (p_in[under] * g_under, below_y(p, None if halo is None else halo[3, here]), below_z(p, g_lo))
        for d in range(3):
            v, h = v_in[d, here], None if halo is None else halo[d, here]
            total = (v_in[d, under] * g_under + v_in[d, over] * g_over) + (below_y(v, h) + above_y(v, h))
            total = total + (below_z(v, g_lo) + above_z(v, g_hi)) - 6.0 * v
            v_out[d, here] = v + scale * (force_ref[d] + total - (p - p_below[d]))

    def divergence_planes(x, n, v_in, halo_y):
        here, over = planes(x, n), planes(x + 1, n)
        vx, vy, vz = v_in[0, here], v_in[1, here], v_in[2, here]
        total = (v_in[0, over] * gate_x[over] - vx) + (above_y(vy, halo_y[here]) - vy) + (above_z(vz, gate_hi[here]) - vz)
        return ext[4, here] * total

    step, shape3 = 5, (5, 8, 128)
    sub3, lane3 = iotas(shape3)
    for x in range(1, 31, step):
        velocity_planes(x, step, ext, ext.at[3], None, vel1)
        if x == 1:
            hear(0)
            tell(1, 2)

    for copy in faces:
        copy.wait()

    row_lo, row_hi = ext[5, OFF - 1], ext[5, OFF + TILE]

    def spread_lo(tile):
        return jnp.where(lane < 64, tile, roll(tile, 64, 1))

    def spread_hi(tile):
        half = jnp.where(lane >= 96, tile, roll(tile, 96, 1))
        return jnp.where(lane >= 64, half, roll(half, 64, 1))

    corners = [recv_corner[k] for k in range(4)]
    col_lo, col_hi = spread_lo(recv_lo[2, 0:8]), spread_hi(recv_hi[1, 0:8])
    z_lo_outer = [(flag(corners[k], 6), flag(col, 4), flag(corners[k + 1], 6)) for k, col in ((0, col_lo), (2, col_hi))]
    z_hi_outer = [(flag(corners[k], 7), flag(col, 5), flag(corners[k + 1], 7)) for k, col in ((0, col_lo), (2, col_hi))]
    mid = [row_lo, own, row_hi]
    for k, x, n in ((0, OFF - 2, 2), (2, OFF + TILE, 3)):
        gate_lo[pl.ds(x, n)] = jnp.broadcast_to(jnp.where(depth == 0, flag(mid[k], 4), one)[None], (n, 8, 128))
        gate_hi[pl.ds(x, n)] = jnp.broadcast_to(jnp.where(depth == TILE - 1, flag(mid[k], 5), one)[None], (n, 8, 128))

    def by_region(tiles):
        return jnp.concatenate([tiles[0]] + [tiles[1]] * 4 + [tiles[2]], axis=0)

    def strip_gates(side, col, is_own, crossing, d):
        z_lo, z_hi, cross = [], [], []
        for k in range(3):
            z_lo.append(jnp.where(depth == 0, jnp.where(is_own, flag(mid[k], 4), z_lo_outer[side][k]), one))
            z_hi.append(jnp.where(depth == TILE - 1, jnp.where(is_own, flag(mid[k], 5), z_hi_outer[side][k]), one))
            cross.append(jnp.where(crossing, flag(mid[k], d), one))
        x_lo = jnp.where(sub == 0, jnp.where(is_own, flag(own, 0), flag(col, 0)), one)
        x_hi = jnp.where(sub == 0, jnp.where(is_own, flag(own, 1), flag(col, 1)), one)
        x_gate = jnp.concatenate([one, x_lo, one, one, one, x_hi], axis=0)
        return x_gate, by_region(cross), by_region(z_lo), by_region(z_hi)

    lo_gates = strip_gates(0, col_lo, lane >= 64, lane // TILE == 2, 2)
    hi_gates = strip_gates(1, col_hi, lane < 32, lane // TILE == 1, 3)
    cross_lo = by_region([flag(tile, 2) for tile in mid])
    cross_hi = by_region([flag(tile, 3) for tile in mid])

    def strip(received, tiles, g):
        return jnp.concatenate([roll(tiles[0], 6 - 2 * g, 0), received[g], roll(tiles[1], -2 * g, 0)], axis=0)

    raw = [strip(recv_lo, corners[:2], g) for g in range(3)]
    outer = [roll(raw[0], 64, 1), raw[0], roll(raw[1], 64, 1), raw[1], roll(raw[2], 64, 1)]
    lo = [jnp.where(lane_long < 64, outer[f], roll(ext[f, :, 0, :], 64, 1)) for f in range(5)]
    raw = [strip(recv_hi, corners[2:], g) for g in range(3)]
    outer = [roll(raw[0], 32, 1), roll(raw[1], 32, 1), roll(raw[0], 96, 1), roll(raw[2], 32, 1), roll(raw[2], 96, 1)]
    hi = [jnp.where(lane_long < 32, roll(ext[f, :, 7, :], 32, 1), outer[f]) for f in range(5)]

    depth_long = lane_long % TILE

    def strip_below(v, gates):
        x_gate, y_gate, z_lo, _ = gates
        return (
            roll(v, 1, 0) * x_gate,
            roll(v, 32, 1) * y_gate,
            jnp.where(depth_long == 0, roll(v, -31, 1), roll(v, 1, 1)) * z_lo,
        )

    def strip_above(v, gates):
        x_gate, y_gate, _, z_hi = gates
        return (
            roll(v * x_gate, -1, 0),
            roll(v * y_gate, -32, 1),
            jnp.where(depth_long == TILE - 1, roll(v, 31, 1), roll(v, -1, 1)) * z_hi,
        )

    def strip_velocity(v, p, m, gates, wanted):
        under = strip_below(p, gates)
        result = []
        for d in wanted:
            b, a = strip_below(v[d], gates), strip_above(v[d], gates)
            laplace = (b[0] + a[0]) + (b[1] + a[1]) + (b[2] + a[2]) - 6.0 * v[d]
            result.append(v[d] + RATE * m * (force_ref[d] + laplace - (p - under[d])))
        return result

    def strip_pressure(v, p, m, gates):
        total = zero_strip
        for d in range(3):
            total = total + (strip_above(v[d], gates)[d] - v[d])
        return p + PRESSURE_RATE * (m * total)

    zero_strip = jnp.zeros((PLANES, 128), f32)

    def put_lo(dst, v):
        dst[:, 0, :] = roll(v, 64, 1) * cross_lo

    def put_hi(dst, v):
        dst[:, 7, :] = roll(v, 96, 1) * cross_hi

    lo1 = strip_velocity(lo[:3], lo[3], lo[4], lo_gates, (0, 1, 2))
    hi1 = strip_velocity(hi[:3], hi[3], hi[4], hi_gates, (0, 1, 2))
    for d in range(3):
        put_lo(halo1.at[d], lo1[d])
        put_hi(halo1.at[d], hi1[d])
    lo_p1 = strip_pressure(lo1, lo[3], lo[4], lo_gates)
    hi_p1 = strip_pressure(hi1, hi[3], hi[4], hi_gates)
    put_lo(halo1.at[3], lo_p1)

    for x, step in ((-1, 2), (31, 3)):
        sub3, lane3 = iotas((step, 8, 128))
        velocity_planes(x, step, ext, ext.at[3], None, vel1)
    scale_lo, scale_hi = RATE * ext[4, :, 0, :], RATE * ext[4, :, 7, :]
    for d in range(3):
        face = lo[d] + lo[3] if d == 1 else lo[d]
        vel1[d, :, 0, :] = vel1[d, :, 0, :] + jnp.where(lane_long < 32, scale_lo * (roll(face, 96, 1) * cross_lo), 0.0)
        vel1[d, :, 7, :] = vel1[d, :, 7, :] + jnp.where(lane_long >= 96, scale_hi * (roll(hi[d], 64, 1) * cross_hi), 0.0)

    hear(1)
    tell(2, 4)
    tell(3, 1)

    step = 5
    sub3, lane3 = iotas((step, 8, 128))
    for x in range(-1, 32, step):
        pres1[planes(x, step)] = ext[3, planes(x, step)] + PRESSURE_RATE * divergence_planes(x, step, vel1, halo1.at[1])

    hi1 = [jnp.where(lane_long < 32, roll(vel1[d, :, 7, :], 32, 1), hi1[d]) for d in range(3)]
    hi_p1 = jnp.where(lane_long < 32, roll(pres1[:, 7, :], 32, 1), hi_p1)
    put_hi(halo2, strip_velocity(hi1, hi_p1, hi[4], hi_gates, (1,))[0])

    step = 3
    sub3, lane3 = iotas((step, 8, 128))
    for x in range(0, 33, step):
        velocity_planes(x, step, vel1, pres1, halo1, vel2)

    step = 8
    sub3, lane3 = iotas((step, 8, 128))
    message = zero
    for x in range(0, TILE, step):
        div = divergence_planes(x, step, vel2, halo2)
        pres2[pl.ds(x, step)] = pres1[planes(x, step)] + PRESSURE_RATE * div
        part = jnp.sum(div, axis=0)
        for shift in (1, 2, 4):
            part = part + jnp.where((lane // shift) % 2 == 0, roll(part, -shift, 1), roll(part, shift, 1))
        part = part + roll(part, 32, 1)
        part = part + roll(part, 64, 1)
        part = part + jnp.where(sub % 2 == 0, roll(part, -1, 0), roll(part, 1, 0))
        message = jnp.where(jnp.logical_and(2 * (lane // 32) + (lane % 8) // 4 == x // 8, sub == 2 * (lane % 4)), part, message)
    table[0, z_count // 2] = jnp.sum(message, axis=0, keepdims=True)[:, :64] * (1.0 / 64.0)

    hear(3)
    middle = z_count // 2
    near = []
    for k in range(1, NEAR + 1):
        for sign in (1, -1):
            index = len(near)
            near.append(pltpu.make_async_remote_copy(
                src_ref=table.at[0, middle], dst_ref=table.at[0, middle - sign * k], send_sem=gsend_sem.at[index], recv_sem=grecv_sem.at[index],
                device_id=along(0, sign * k), device_id_type=MESH))
    for copy in reversed(near):
        copy.start()

    stores = []
    for s in range(8):
        lanes = pl.ds(128 * s, 128)
        stores.append(pltpu.make_async_copy(vel2.at[:, pl.ds(OFF, TILE), s], fields_out.at[pl.ds(0, 3), :, lanes], store_sem.at[s]))
        stores.append(pltpu.make_async_copy(pres2.at[:, s], fields_out.at[3, :, lanes], store_sem.at[8 + s]))
    for copy in stores:
        copy.start()

    hear(2)
    tell(4, 3)
    hear(5)

    def copies(pairs):
        result = []
        for src, dst, device in pairs:
            index = next(counter)
            result.append(pltpu.make_async_remote_copy(
                src_ref=src, dst_ref=dst, send_sem=gsend_sem.at[index], recv_sem=grecv_sem.at[index], device_id=device, device_id_type=MESH))
            result[-1].start()
        return result

    counter = iter(range(len(near), GATHER_COPIES))
    for copy in near:
        copy.wait()
    hear(4)
    width = 2 * NEAR + 1
    block, below_block, above_block = pl.ds(middle - NEAR, width), pl.ds(0, width), pl.ds(2 * FAR, width)
    far = copies([(table.at[0, block], table.at[0, below_block], along(0, FAR)), (table.at[0, block], table.at[0, above_block], along(0, -FAR))])
    across = copies([(table.at[0, block], table.at[y_count - j, block], along(j, 0)) for j in range(1, y_count)])
    for copy in far:
        copy.wait()
    across += copies([(table.at[0, part], table.at[y_count - j, part], along(j, 0)) for j in range(1, y_count) for part in (below_block, above_block)])

    spot = lax.broadcasted_iota(jnp.int32, (64, 512), 1)
    entry = spot // 128 % 2 * 32 + spot % 4 * 8 + spot // 64 % 2 * 4 + spot // 8 % 4
    pick = jnp.where(lax.broadcasted_iota(jnp.int32, (64, 512), 0) == entry, 1.0, 0.0).astype(f32)
    spot = lax.broadcasted_iota(jnp.int32, (8, 512), 1)
    octant = spot // 256 * 4 + (spot // 32) % 2 * 2 + (spot // 4) % 2
    holds = lax.broadcasted_iota(jnp.int32, (8, 512), 0) == octant

    for copy in across:
        copy.wait()
    for o in range(8):
        source = source_ref[0, o]
        kept = jnp.maximum(source, 0)
        dy = lax.rem(kept // z_count - y + y_count, y_count)
        dz = lax.rem(lax.rem(kept, z_count) - z + z_count + middle, z_count)
        taken = table[dy, dz]
        row_buf[pl.ds(o, 1), :] = jnp.where(source >= 0, taken, jnp.zeros_like(taken))
    spread = jnp.dot(row_buf[...], pick, preferred_element_type=f32, precision=lax.Precision.HIGHEST)
    coarse_out[...] = jnp.sum(jnp.where(holds, spread, 0.0), axis=0, keepdims=True)

    for copy in stores:
        copy.wait()


def on_device(rows, fields, fluid_mask, body_force, neighbours, sources):
    y_count, z_count = 4, 32
    f32 = jnp.float32
    volume = lambda n: pltpu.VMEM((n, PLANES, 8, 128), f32)
    planes = lambda: pltpu.VMEM((PLANES, 8, 128), f32)
    any_space = pl.BlockSpec(memory_space=pl.ANY)
    hbm = pl.BlockSpec(memory_space=pltpu.HBM)
    new_fields, coarse = pl.pallas_call(
        functools.partial(kernel, rows, y_count, z_count),
        out_shape=(
            jax.ShapeDtypeStruct((4, TILE, TILE * TILE), f32),
            jax.ShapeDtypeStruct((1, 512), f32),
        ),
        in_specs=[hbm] * 5,
        out_specs=(any_space, pl.BlockSpec(memory_space=pltpu.VMEM)),
        scratch_shapes=[
            pltpu.SMEM((1, 6), jnp.int32),
            pltpu.SMEM((1, 8), jnp.int32),
            pltpu.SMEM((3,), f32),
            volume(6),
            pltpu.VMEM((TILE, 8, 128), jnp.int32),
            volume(3),
            planes(),
            volume(3),
            pltpu.VMEM((TILE, 8, 128), f32),
            volume(4),
            planes(),
            planes(),
            planes(),
            planes(),
            pltpu.VMEM((3, TILE, 128), f32),
            pltpu.VMEM((3, TILE, 128), f32),
            pltpu.VMEM((3, TILE, 128), f32),
            pltpu.VMEM((3, TILE, 128), f32),
            pltpu.VMEM((4, 8, 128), f32),
            pltpu.VMEM((4, 8, 128), f32),
            pltpu.VMEM((y_count, SLOTS, 1, 64), f32),
            pltpu.VMEM((8, 64), f32),
            pltpu.SemaphoreType.DMA((19,)),
            pltpu.SemaphoreType.DMA((16,)),
            pltpu.SemaphoreType.DMA((8,)),
            pltpu.SemaphoreType.DMA((8,)),
            pltpu.SemaphoreType.DMA((GATHER_COPIES,)),
            pltpu.SemaphoreType.DMA((GATHER_COPIES,)),
            pltpu.SemaphoreType.REGULAR((6,)),
        ],
        compiler_params=pltpu.CompilerParams(
            collective_id=0, has_side_effects=True, vmem_limit_bytes=32 * 1024 * 1024
        ),
    )(
        *(
            pltpu.with_memory_space_constraint(array, pltpu.HBM)
            for array in (
                neighbours,
                sources,
                body_force,
                fields.reshape(4, TILE, TILE * TILE),
                fluid_mask.reshape(TILE, TILE * TILE),
            )
        )
    )
    return new_fields[None], coarse


def solution(mesh):
    return jax.shard_map(
        functools.partial(on_device, mesh.shape["row"]),
        mesh=mesh,
        in_specs=(
            P(("row", "col"), None, None, None),
            P(("row", "col"), None, None),
            P(),
            P(("row", "col"), None),
            P(("row", "col"), None),
        ),
        out_specs=(P(("row", "col"), None, None, None), P(("row", "col"), None)),
        check_vma=False,
    )
```

time: 52.1 us -> 48.4 us (0.929)
  the two profiles are of different devices: /device:TPU:2 before, /device:TPU:4 now
where the time goes in v2:
time: 48.4 us; the launch traced here: 48.2 us
  Pallas kernels  46.2 us (95%)
  local copies, waits for them, and re-layouts  1.37 us (3%)
  between operations  0.64 us (1%)
    pallas_call x1, Pallas kernels, on_device(): pl.pallas_call(functools.partial(kernel, rows, y_count, z_count), out_sha...  46.2 us
    unnamed x2, local copies, waits for them, and re-layouts  1.37 us

profile of v2, /device:TPU:4, one launch (start us, length us, event | category | flops | bytes accessed | tf_op | source)
XLA Modules:
  0.0 48.2 jit_solution(16402250324775843894)
XLA Ops:
  0.6 46.2 %shard_map.68 = (f32[4,32,1024]{2,1,0:T(8,128)S(1)}, f32[1,512]{1,0:T(1,128)S(1)}) custom-call(s32[1,6]{1,0:T(1,128)} %neighbour_hbm.1, s32[1,8]{1,0:T(1,128)} %source_hbm.1, f32[3]{0:T(128)} %force_hbm.1, f32[4,32,1024]{2,1,0:T(8,128)} %bitcast.4, s32[32,1024]{1,0:T(8,128)} %bitcast.5), custom_call_target="tpu_custom_call" | custom-call | tf_op jit(solution)/shard_map/pallas_call | solution.py:418
  46.9 0.8 %copy.9 = f32[1,4,32,1024]{3,2,1,0:T(8,128)} copy(f32[1,4,32,1024]{3,2,1,0:T(8,128)S(1)} %bitcast.3) | data formatting | bytes 1048576
  47.7 0.6 %copy.10 = f32[1,512]{1,0:T(1,128)} copy(f32[1,512]{1,0:T(1,128)S(1)} %get-tuple-element.9) | data formatting | bytes 4096

commit v3 on v2

--- a/solution.py
+++ b/solution.py
@@ -17,6 +17,7 @@
 FAR = 11
 SLOTS = 33
 GATHER_COPIES = 2 * NEAR + 2 + 9
+DIRECT = 4
 
 
 def roll(values, shift, axis):
@@ -28,8 +29,8 @@
     neighbour_hbm, source_hbm, force_hbm, fields_ref, mask_ref, fields_out, coarse_out,
     neighbour_ref, source_ref, force_ref,
     ext, mask_raw, vel1, pres1, vel2, pres2, halo1, halo2, gate_x, gate_lo, gate_hi,
-    send_lo, send_hi, recv_lo, recv_hi, send_corner, recv_corner, table, row_buf,
-    load_sem, store_sem, send_sem, recv_sem, gsend_sem, grecv_sem, know_sem,
+    send_lo, send_hi, recv_lo, recv_hi, send_corner, recv_corner, table, straight, row_buf,
+    load_sem, store_sem, send_sem, recv_sem, gsend_sem, grecv_sem, dsend_sem, drecv_sem, know_sem,
 ):
     f32 = jnp.float32
     cols = y_count * z_count
@@ -49,6 +50,18 @@
     barrier = pltpu.get_barrier_semaphore()
     for device in greeted:
         pl.semaphore_signal(barrier, inc=1, device_id=device, device_id_type=MESH)
+    is_direct = z < DIRECT
+    is_late = jnp.logical_and(r == 0, c == 0)
+
+    @pl.when(jnp.logical_and(is_direct, jnp.logical_not(is_late)))
+    def _():
+        def greet(k, carry):
+            pl.semaphore_signal(barrier, inc=1, device_id=(r, lax.rem(c + k, cols)), device_id_type=MESH)
+            return carry
+
+        lax.fori_loop(1, cols, greet, 0)
+
+    greetings = len(greeted) + y_count * DIRECT - jnp.where(jnp.logical_and(is_direct, jnp.logical_not(is_late)), 1, 0) - jnp.where(r == 0, 1, 0)
 
     smalls = [
         pltpu.make_async_copy(neighbour_hbm, neighbour_ref, load_sem.at[16]),
@@ -124,7 +137,7 @@
     send_corner[2] = corner(send_lo, 24, 6)
     send_corner[3] = corner(send_lo, 0, 0)
 
-    pl.semaphore_wait(barrier, len(greeted))
+    pl.semaphore_wait(barrier, greetings)
 
     plan = [(send_corner.at[k], recv_corner.at[k], offset) for k, offset in enumerate([(1, 1), (-1, 1), (1, -1), (-1, -1)])]
     plan += [(send_hi, recv_lo, (0, 1)), (send_lo, recv_hi, (0, -1))]
@@ -340,8 +353,32 @@
         message = jnp.where(jnp.logical_and(2 * (lane // 32) + (lane % 8) // 4 == x // 8, sub == 2 * (lane % 4)), part, message)
     table[0, z_count // 2] = jnp.sum(message, axis=0, keepdims=True)[:, :64] * (1.0 / 64.0)
 
+    middle = z_count // 2
+
+    def straight_copy(dy, at):
+        return pltpu.make_async_remote_copy(
+            src_ref=table.at[0, pl.ds(middle, 1)], dst_ref=straight.at[pl.ds(c, 1)], send_sem=dsend_sem.at[dy * DIRECT + at], recv_sem=drecv_sem.at[0],
+            device_id=(r, lax.rem(y + dy, y_count) * z_count + at), device_id_type=MESH)
+
+    def straight_goes(dy, at):
+        goes = z != at if dy == 0 else None
+        if at == 0:
+            awake = jnp.logical_or(r > 0, lax.rem(y + dy, y_count) > 0)
+            goes = awake if goes is None else jnp.logical_and(goes, awake)
+        return goes
+
+    def for_each_straight(act):
+        for dy in (2, 1, y_count - 1, 0):
+            for at in range(DIRECT):
+                goes = straight_goes(dy, at)
+                if goes is None:
+                    act(straight_copy(dy, at))
+                else:
+                    pl.when(goes)(functools.partial(act, straight_copy(dy, at)))
+
+    for_each_straight(lambda copy: copy.start())
+
     hear(3)
-    middle = z_count // 2
     near = []
     for k in range(1, NEAR + 1):
         for sign in (1, -1):
@@ -364,26 +401,41 @@
     tell(4, 3)
     hear(5)
 
-    def copies(pairs):
-        result = []
-        for src, dst, device in pairs:
-            index = next(counter)
-            result.append(pltpu.make_async_remote_copy(
-                src_ref=src, dst_ref=dst, send_sem=gsend_sem.at[index], recv_sem=grecv_sem.at[index], device_id=device, device_id_type=MESH))
-            result[-1].start()
-        return result
-
-    counter = iter(range(len(near), GATHER_COPIES))
     for copy in near:
         copy.wait()
     hear(4)
     width = 2 * NEAR + 1
     block, below_block, above_block = pl.ds(middle - NEAR, width), pl.ds(0, width), pl.ds(2 * FAR, width)
-    far = copies([(table.at[0, block], table.at[0, below_block], along(0, FAR)), (table.at[0, block], table.at[0, above_block], along(0, -FAR))])
-    across = copies([(table.at[0, block], table.at[y_count - j, block], along(j, 0)) for j in range(1, y_count)])
-    for copy in far:
-        copy.wait()
-    across += copies([(table.at[0, part], table.at[y_count - j, part], along(j, 0)) for j in range(1, y_count) for part in (below_block, above_block)])
+    far = []
+    for k, (sign, landed) in enumerate(((1, below_block), (-1, above_block))):
+        far.append(pltpu.make_async_remote_copy(
+            src_ref=table.at[0, block], dst_ref=table.at[0, landed], send_sem=gsend_sem.at[len(near) + k], recv_sem=grecv_sem.at[len(near) + k],
+            device_id=along(0, sign * FAR), device_id_type=MESH))
+    wanted = [lax.rem(z + sign * FAR + z_count, z_count) >= DIRECT for sign in (1, -1)]
+    for copy, needed in zip(far, wanted, strict=True):
+        pl.when(needed)(copy.start)
+
+    def y_copies(parts, first):
+        result = []
+        for j in range(1, y_count):
+            for part in parts:
+                index = first + len(result)
+                result.append(pltpu.make_async_remote_copy(
+                    src_ref=table.at[0, part], dst_ref=table.at[y_count - j, part], send_sem=gsend_sem.at[index], recv_sem=grecv_sem.at[index],
+                    device_id=along(j, 0), device_id_type=MESH))
+        return result
+
+    across = y_copies([block], len(near) + 2)
+    across_far = y_copies([below_block, above_block], len(near) + 2 + len(across))
+
+    @pl.when(jnp.logical_not(is_direct))
+    def _():
+        for copy in across:
+            copy.start()
+        for copy in far:
+            copy.wait_recv()
+        for copy in across_far:
+            copy.start()
 
     spot = lax.broadcasted_iota(jnp.int32, (64, 512), 1)
     entry = spot // 128 % 2 * 32 + spot % 4 * 8 + spot // 64 % 2 * 4 + spot // 8 % 4
@@ -392,20 +444,49 @@
     octant = spot // 256 * 4 + (spot // 32) % 2 * 2 + (spot // 4) % 2
     holds = lax.broadcasted_iota(jnp.int32, (8, 512), 0) == octant
 
-    for copy in across:
-        copy.wait()
-    for o in range(8):
-        source = source_ref[0, o]
-        kept = jnp.maximum(source, 0)
-        dy = lax.rem(kept // z_count - y + y_count, y_count)
-        dz = lax.rem(lax.rem(kept, z_count) - z + z_count + middle, z_count)
-        taken = table[dy, dz]
-        row_buf[pl.ds(o, 1), :] = jnp.where(source >= 0, taken, jnp.zeros_like(taken))
+    for copy, needed in zip(far, wanted, strict=True):
+        pl.when(needed)(copy.wait_send)
+    for_each_straight(lambda copy: copy.wait_send())
+
+    sources = [source_ref[0, o] for o in range(8)]
+    kept = [jnp.maximum(source, 0) for source in sources]
+
+    def keep(o, taken):
+        row_buf[pl.ds(o, 1), :] = jnp.where(sources[o] >= 0, taken, jnp.zeros_like(taken))
+
+    handed = pltpu.make_async_remote_copy(
+        src_ref=straight, dst_ref=straight, send_sem=dsend_sem.at[y_count * DIRECT], recv_sem=drecv_sem.at[1], device_id=(r, 0 * c), device_id_type=MESH)
+    hands_on = jnp.logical_and(r == 0, c == 1)
+
+    @pl.when(jnp.logical_and(is_direct, jnp.logical_not(is_late)))
+    def _():
+        straight[pl.ds(c, 1)] = table[0, pl.ds(middle, 1)]
+        arrived = straight.at[pl.ds(0, cols - 1)]
+        pltpu.make_async_copy(arrived, arrived, drecv_sem.at[0]).wait()
+
+    pl.when(hands_on)(handed.start)
+    pl.when(is_late)(handed.wait_recv)
+
+    @pl.when(is_direct)
+    def _():
+        for o in range(8):
+            keep(o, straight[kept[o]])
+
+    @pl.when(jnp.logical_not(is_direct))
+    def _():
+        for copy in across + across_far:
+            copy.wait()
+        for o in range(8):
+            dy = lax.rem(kept[o] // z_count - y + y_count, y_count)
+            dz = lax.rem(lax.rem(kept[o], z_count) - z + z_count + middle, z_count)
+            keep(o, table[dy, dz])
+
     spread = jnp.dot(row_buf[...], pick, preferred_element_type=f32, precision=lax.Precision.HIGHEST)
     coarse_out[...] = jnp.sum(jnp.where(holds, spread, 0.0), axis=0, keepdims=True)
 
     for copy in stores:
         copy.wait()
+    pl.when(hands_on)(handed.wait_send)
 
 
 def on_device(rows, fields, fluid_mask, body_force, neighbours, sources):
@@ -445,6 +526,7 @@
             pltpu.VMEM((4, 8, 128), f32),
             pltpu.VMEM((4, 8, 128), f32),
             pltpu.VMEM((y_count, SLOTS, 1, 64), f32),
+            pltpu.VMEM((y_count * z_count, 1, 64), f32),
             pltpu.VMEM((8, 64), f32),
             pltpu.SemaphoreType.DMA((19,)),
             pltpu.SemaphoreType.DMA((16,)),
@@ -452,6 +534,8 @@
             pltpu.SemaphoreType.DMA((8,)),
             pltpu.SemaphoreType.DMA((GATHER_COPIES,)),
             pltpu.SemaphoreType.DMA((GATHER_COPIES,)),
+            pltpu.SemaphoreType.DMA((y_count * DIRECT + 1,)),
+            pltpu.SemaphoreType.DMA((2,)),
             pltpu.SemaphoreType.REGULAR((6,)),
         ],
         compiler_params=pltpu.CompilerParams(

time: 48.4 us -> 45.4 us (0.938)
  the two profiles are of different devices: /device:TPU:4 before, /device:TPU:128 now
where the time goes in v3:
time: 45.4 us; the launch traced here: 45.2 us
  Pallas kernels  43.2 us (95%)
  local copies, waits for them, and re-layouts  1.37 us (3%)
  between operations  0.64 us (1%)
    pallas_call x1, Pallas kernels, on_device(): pl.pallas_call(functools.partial(kernel, rows, y_count, z_count), out_sha...  43.2 us
    unnamed x2, local copies, waits for them, and re-layouts  1.37 us

profile of v3, /device:TPU:128, one launch (start us, length us, event | category | flops | bytes accessed | tf_op | source)
XLA Modules:
  0.0 45.2 jit_solution(18100070781820221568)
XLA Ops:
  0.6 43.2 %shard_map.68 = (f32[4,32,1024]{2,1,0:T(8,128)S(1)}, f32[1,512]{1,0:T(1,128)S(1)}) custom-call(s32[1,6]{1,0:T(1,128)} %neighbour_hbm.1, s32[1,8]{1,0:T(1,128)} %source_hbm.1, f32[3]{0:T(128)} %force_hbm.1, f32[4,32,1024]{2,1,0:T(8,128)} %bitcast.4, s32[32,1024]{1,0:T(8,128)} %bitcast.5), custom_call_target="tpu_custom_call" | custom-call | tf_op jit(solution)/shard_map/pallas_call | solution.py:499
  43.8 0.8 %copy.9 = f32[1,4,32,1024]{3,2,1,0:T(8,128)} copy(f32[1,4,32,1024]{3,2,1,0:T(8,128)S(1)} %bitcast.3) | data formatting | bytes 1048576
  44.6 0.6 %copy.10 = f32[1,512]{1,0:T(1,128)} copy(f32[1,512]{1,0:T(1,128)S(1)} %get-tuple-element.9) | data formatting | bytes 4096

commit v4 on v3

--- a/solution.py
+++ b/solution.py
@@ -18,6 +18,7 @@
 SLOTS = 33
 GATHER_COPIES = 2 * NEAR + 2 + 9
 DIRECT = 4
+MID = 7
 
 
 def roll(values, shift, axis):
@@ -61,7 +62,17 @@
 
         lax.fori_loop(1, cols, greet, 0)
 
-    greetings = len(greeted) + y_count * DIRECT - jnp.where(jnp.logical_and(is_direct, jnp.logical_not(is_late)), 1, 0) - jnp.where(r == 0, 1, 0)
+    is_mid = jnp.logical_and(z >= DIRECT, z < MID)
+
+    @pl.when(is_mid)
+    def _():
+        def greet(k, carry):
+            pl.semaphore_signal(barrier, inc=1, device_id=(r, y * z_count + lax.rem(z + k, z_count)), device_id_type=MESH)
+            return carry
+
+        lax.fori_loop(1, z_count, greet, 0)
+
+    greetings = len(greeted) + y_count * DIRECT - jnp.where(jnp.logical_and(is_direct, jnp.logical_not(is_late)), 1, 0) - jnp.where(r == 0, 1, 0) + MID - DIRECT - jnp.where(is_mid, 1, 0)
 
     smalls = [
         pltpu.make_async_copy(neighbour_hbm, neighbour_ref, load_sem.at[16]),
@@ -357,7 +368,7 @@
 
     def straight_copy(dy, at):
         return pltpu.make_async_remote_copy(
-            src_ref=table.at[0, pl.ds(middle, 1)], dst_ref=straight.at[pl.ds(c, 1)], send_sem=dsend_sem.at[dy * DIRECT + at], recv_sem=drecv_sem.at[0],
+            src_ref=table.at[0, pl.ds(middle, 1)], dst_ref=straight.at[pl.ds(c, 1)], send_sem=dsend_sem.at[dy * MID + at], recv_sem=drecv_sem.at[0],
             device_id=(r, lax.rem(y + dy, y_count) * z_count + at), device_id_type=MESH)
 
     def straight_goes(dy, at):
@@ -369,7 +380,7 @@
 
     def for_each_straight(act):
         for dy in (2, 1, y_count - 1, 0):
-            for at in range(DIRECT):
+            for at in range(MID if dy == 0 else DIRECT):
                 goes = straight_goes(dy, at)
                 if goes is None:
                     act(straight_copy(dy, at))
@@ -411,7 +422,7 @@
         far.append(pltpu.make_async_remote_copy(
             src_ref=table.at[0, block], dst_ref=table.at[0, landed], send_sem=gsend_sem.at[len(near) + k], recv_sem=grecv_sem.at[len(near) + k],
             device_id=along(0, sign * FAR), device_id_type=MESH))
-    wanted = [lax.rem(z + sign * FAR + z_count, z_count) >= DIRECT for sign in (1, -1)]
+    wanted = [lax.rem(z + sign * FAR + z_count, z_count) >= MID for sign in (1, -1)]
     for copy, needed in zip(far, wanted, strict=True):
         pl.when(needed)(copy.start)
 
@@ -428,7 +439,7 @@
     across = y_copies([block], len(near) + 2)
     across_far = y_copies([below_block, above_block], len(near) + 2 + len(across))
 
-    @pl.when(jnp.logical_not(is_direct))
+    @pl.when(z >= MID)
     def _():
         for copy in across:
             copy.start()
@@ -454,25 +465,42 @@
     def keep(o, taken):
         row_buf[pl.ds(o, 1), :] = jnp.where(sources[o] >= 0, taken, jnp.zeros_like(taken))
 
+    def arrive(count):
+        straight[pl.ds(c, 1)] = table[0, pl.ds(middle, 1)]
+        arrived = straight.at[pl.ds(0, count)]
+        pltpu.make_async_copy(arrived, arrived, drecv_sem.at[0]).wait()
+
     handed = pltpu.make_async_remote_copy(
-        src_ref=straight, dst_ref=straight, send_sem=dsend_sem.at[y_count * DIRECT], recv_sem=drecv_sem.at[1], device_id=(r, 0 * c), device_id_type=MESH)
-    hands_on = jnp.logical_and(r == 0, c == 1)
+        src_ref=straight, dst_ref=straight, send_sem=dsend_sem.at[y_count * MID], recv_sem=drecv_sem.at[1], device_id=(r, 0 * c), device_id_type=MESH)
+    hands_on = jnp.logical_and(r == 0, c == cols - z_count + MID - 1)
 
     @pl.when(jnp.logical_and(is_direct, jnp.logical_not(is_late)))
     def _():
-        straight[pl.ds(c, 1)] = table[0, pl.ds(middle, 1)]
-        arrived = straight.at[pl.ds(0, cols - 1)]
-        pltpu.make_async_copy(arrived, arrived, drecv_sem.at[0]).wait()
+        arrive(cols - 1)
+
+    @pl.when(is_mid)
+    def _():
+        arrive(z_count - 1)
+        ring = straight.at[pl.ds(y * z_count, z_count)]
+        shares = [
+            pltpu.make_async_remote_copy(
+                src_ref=ring, dst_ref=ring, send_sem=dsend_sem.at[y_count * MID + j], recv_sem=drecv_sem.at[1 + j], device_id=along(j, 0), device_id_type=MESH)
+            for j in range(1, y_count)
+        ]
+        for copy in shares:
+            copy.start()
+        for copy in shares:
+            copy.wait()
 
     pl.when(hands_on)(handed.start)
     pl.when(is_late)(handed.wait_recv)
 
-    @pl.when(is_direct)
+    @pl.when(z < MID)
     def _():
         for o in range(8):
             keep(o, straight[kept[o]])
 
-    @pl.when(jnp.logical_not(is_direct))
+    @pl.when(z >= MID)
     def _():
         for copy in across + across_far:
             copy.wait()
@@ -534,8 +562,8 @@
             pltpu.SemaphoreType.DMA((8,)),
             pltpu.SemaphoreType.DMA((GATHER_COPIES,)),
             pltpu.SemaphoreType.DMA((GATHER_COPIES,)),
-            pltpu.SemaphoreType.DMA((y_count * DIRECT + 1,)),
-            pltpu.SemaphoreType.DMA((2,)),
+            pltpu.SemaphoreType.DMA((y_count * MID + y_count,)),
+            pltpu.SemaphoreType.DMA((1 + y_count,)),
             pltpu.SemaphoreType.REGULAR((6,)),
         ],
         compiler_params=pltpu.CompilerParams(

time: 45.4 us -> 44.8 us (0.987)
  the two profiles are of different devices: /device:TPU:128 before, /device:TPU:1 now
where the time goes in v4:
time: 44.8 us; the launch traced here: 44.6 us
  Pallas kernels  42.6 us (95%)
  local copies, waits for them, and re-layouts  1.37 us (3%)
  between operations  0.64 us (1%)
    pallas_call x1, Pallas kernels, on_device(): pl.pallas_call(functools.partial(kernel, rows, y_count, z_count), out_sha...  42.6 us
    unnamed x2, local copies, waits for them, and re-layouts  1.37 us

profile of v4, /device:TPU:1, one launch (start us, length us, event | category | flops | bytes accessed | tf_op | source)
XLA Modules:
  0.0 44.6 jit_solution(4096050855573305083)
XLA Ops:
  0.6 42.6 %shard_map.68 = (f32[4,32,1024]{2,1,0:T(8,128)S(1)}, f32[1,512]{1,0:T(1,128)S(1)}) custom-call(s32[1,6]{1,0:T(1,128)} %neighbour_hbm.1, s32[1,8]{1,0:T(1,128)} %source_hbm.1, f32[3]{0:T(128)} %force_hbm.1, f32[4,32,1024]{2,1,0:T(8,128)} %bitcast.4, s32[32,1024]{1,0:T(8,128)} %bitcast.5), custom_call_target="tpu_custom_call" | custom-call | tf_op jit(solution)/shard_map/pallas_call | solution.py:527
  43.3 0.8 %copy.9 = f32[1,4,32,1024]{3,2,1,0:T(8,128)} copy(f32[1,4,32,1024]{3,2,1,0:T(8,128)S(1)} %bitcast.3) | data formatting | bytes 1048576
  44.1 0.6 %copy.10 = f32[1,512]{1,0:T(1,128)} copy(f32[1,512]{1,0:T(1,128)S(1)} %get-tuple-element.9) | data formatting | bytes 4096

commit v5 on v4

--- a/solution.py
+++ b/solution.py
@@ -29,7 +29,7 @@
     rows, y_count, z_count,
     neighbour_hbm, source_hbm, force_hbm, fields_ref, mask_ref, fields_out, coarse_out,
     neighbour_ref, source_ref, force_ref,
-    ext, mask_raw, vel1, pres1, vel2, pres2, halo1, halo2, gate_x, gate_lo, gate_hi,
+    ext, mask_raw, vel1, pres1, vel2, pres2, halo2, gate_x, gate_lo, gate_hi,
     send_lo, send_hi, recv_lo, recv_hi, send_corner, recv_corner, table, straight, row_buf,
     load_sem, store_sem, send_sem, recv_sem, gsend_sem, grecv_sem, dsend_sem, drecv_sem, know_sem,
 ):
@@ -211,7 +211,7 @@
     def divergence_planes(x, n, v_in, halo_y):
         here, over = planes(x, n), planes(x + 1, n)
         vx, vy, vz = v_in[0, here], v_in[1, here], v_in[2, here]
-        total = (v_in[0, over] * gate_x[over] - vx) + (above_y(vy, halo_y[here]) - vy) + (above_z(vz, gate_hi[here]) - vz)
+        total = (v_in[0, over] * gate_x[over] - vx) + (above_y(vy, None if halo_y is None else halo_y[here]) - vy) + (above_z(vz, gate_hi[here]) - vz)
         return ext[4, here] * total
 
     step, shape3 = 5, (5, 8, 128)
@@ -221,6 +221,13 @@
         if x == 1:
             hear(0)
             tell(1, 2)
+    for x, step in ((1, 5), (6, 5), (11, 5), (16, 5), (21, 5), (26, 4)):
+        sub3, lane3 = iotas((step, 8, 128))
+        pres1[planes(x, step)] = ext[3, planes(x, step)] + PRESSURE_RATE * divergence_planes(x, step, vel1, None)
+    step = 4
+    sub3, lane3 = iotas((step, 8, 128))
+    for x in range(2, 30, step):
+        velocity_planes(x, step, vel1, pres1, None, vel2)
 
     for copy in faces:
         copy.wait()
@@ -307,20 +314,13 @@
 
     zero_strip = jnp.zeros((PLANES, 128), f32)
 
-    def put_lo(dst, v):
-        dst[:, 0, :] = roll(v, 64, 1) * cross_lo
-
     def put_hi(dst, v):
         dst[:, 7, :] = roll(v, 96, 1) * cross_hi
 
     lo1 = strip_velocity(lo[:3], lo[3], lo[4], lo_gates, (0, 1, 2))
     hi1 = strip_velocity(hi[:3], hi[3], hi[4], hi_gates, (0, 1, 2))
-    for d in range(3):
-        put_lo(halo1.at[d], lo1[d])
-        put_hi(halo1.at[d], hi1[d])
     lo_p1 = strip_pressure(lo1, lo[3], lo[4], lo_gates)
     hi_p1 = strip_pressure(hi1, hi[3], hi[4], hi_gates)
-    put_lo(halo1.at[3], lo_p1)
 
     for x, step in ((-1, 2), (31, 3)):
         sub3, lane3 = iotas((step, 8, 128))
@@ -335,19 +335,57 @@
     tell(2, 4)
     tell(3, 1)
 
-    step = 5
-    sub3, lane3 = iotas((step, 8, 128))
-    for x in range(-1, 32, step):
-        pres1[planes(x, step)] = ext[3, planes(x, step)] + PRESSURE_RATE * divergence_planes(x, step, vel1, halo1.at[1])
-
-    hi1 = [jnp.where(lane_long < 32, roll(vel1[d, :, 7, :], 32, 1), hi1[d]) for d in range(3)]
+    for x, step in ((-1, 2), (30, 3)):
+        sub3, lane3 = iotas((step, 8, 128))
+        pres1[planes(x, step)] = ext[3, planes(x, step)] + PRESSURE_RATE * divergence_planes(x, step, vel1, None)
+
+    x_own = jnp.concatenate([one, jnp.where(sub == 0, flag(own, 0), one), one, one, one, jnp.where(sub == 0, flag(own, 1), one)], axis=0)
+    z_lo_own = by_region([jnp.where(depth == 0, flag(tile, 4), one) for tile in mid])
+    z_hi_own = by_region([jnp.where(depth == TILE - 1, flag(tile, 5), one) for tile in mid])
+
+    def edge_below(v, under_y):
+        return (
+            roll(v, 1, 0) * x_own,
+            jnp.where(lane_long < 32, under_y, roll(v, 32, 1)),
+            jnp.where(depth_long == 0, roll(v, -31, 1), roll(v, 1, 1)) * z_lo_own,
+        )
+
+    def edge_above(v, over_y):
+        return (
+            roll(v * x_own, -1, 0),
+            jnp.where(lane_long >= 96, over_y, roll(v, -32, 1)),
+            jnp.where(depth_long == TILE - 1, roll(v, 31, 1), roll(v, -1, 1)) * z_hi_own,
+        )
+
+    def over_edge(ref, strip_values, s):
+        return roll(ref[:, 1, :], 96, 1) if s == 0 else roll(strip_values, 64, 1) * cross_hi
+
+    def under_edge(ref, strip_values, s):
+        return roll(strip_values, 96, 1) * cross_lo if s == 0 else roll(ref[:, 6, :], 32, 1)
+
+    for s in (0, 7):
+        total = zero_strip
+        for d in range(3):
+            v = vel1[d, :, s, :]
+            total = total + (edge_above(v, over_edge(vel1.at[d], hi1[d], s))[d] - v)
+        pres1[:, s, :] = ext[3, :, s, :] + PRESSURE_RATE * (ext[4, :, s, :] * total)
+
+    hi1_full = [jnp.where(lane_long < 32, roll(vel1[d, :, 7, :], 32, 1), hi1[d]) for d in range(3)]
     hi_p1 = jnp.where(lane_long < 32, roll(pres1[:, 7, :], 32, 1), hi_p1)
-    put_hi(halo2, strip_velocity(hi1, hi_p1, hi[4], hi_gates, (1,))[0])
-
-    step = 3
-    sub3, lane3 = iotas((step, 8, 128))
-    for x in range(0, 33, step):
-        velocity_planes(x, step, vel1, pres1, halo1, vel2)
+    put_hi(halo2, strip_velocity(hi1_full, hi_p1, hi[4], hi_gates, (1,))[0])
+
+    for x, step in ((0, 2), (30, 3)):
+        sub3, lane3 = iotas((step, 8, 128))
+        velocity_planes(x, step, vel1, pres1, None, vel2)
+    for s in (0, 7):
+        p, scale = pres1[:, s, :], RATE * ext[4, :, s, :]
+        p_below = edge_below(p, under_edge(pres1, lo_p1, s))
+        for d in range(3):
+            v = vel1[d, :, s, :]
+            b = edge_below(v, under_edge(vel1.at[d], lo1[d], s))
+            a = edge_above(v, over_edge(vel1.at[d], hi1[d], s))
+            laplace = (b[0] + a[0]) + (b[1] + a[1]) + (b[2] + a[2]) - 6.0 * v
+            vel2[d, :, s, :] = v + scale * (force_ref[d] + laplace - (p - p_below[d]))
 
     step = 8
     sub3, lane3 = iotas((step, 8, 128))
@@ -542,7 +580,6 @@
             planes(),
             volume(3),
             pltpu.VMEM((TILE, 8, 128), f32),
-            volume(4),
             planes(),
             planes(),
             planes(),

time: 44.8 us -> 44.5 us (level)
  no operation moved by 1% of the time
where the time goes in v5:
time: 44.5 us; the launch traced here: 44.3 us
  Pallas kernels  42.2 us (95%)
  local copies, waits for them, and re-layouts  1.37 us (3%)
  between operations  0.64 us (1%)
    pallas_call x1, Pallas kernels, on_device(): pl.pallas_call(functools.partial(kernel, rows, y_count, z_count), out_sha...  42.2 us
    unnamed x2, local copies, waits for them, and re-layouts  1.37 us

profile of v5, /device:TPU:1, one launch (start us, length us, event | category | flops | bytes accessed | tf_op | source)
XLA Modules:
  0.0 44.3 jit_solution(6874019754086631390)
XLA Ops:
  0.6 42.2 %shard_map.68 = (f32[4,32,1024]{2,1,0:T(8,128)S(1)}, f32[1,512]{1,0:T(1,128)S(1)}) custom-call(s32[1,6]{1,0:T(1,128)} %neighbour_hbm.1, s32[1,8]{1,0:T(1,128)} %source_hbm.1, f32[3]{0:T(128)} %force_hbm.1, f32[4,32,1024]{2,1,0:T(8,128)} %bitcast.4, s32[32,1024]{1,0:T(8,128)} %bitcast.5), custom_call_target="tpu_custom_call" | custom-call | tf_op jit(solution)/shard_map/pallas_call | solution.py:565
  42.9 0.8 %copy.9 = f32[1,4,32,1024]{3,2,1,0:T(8,128)} copy(f32[1,4,32,1024]{3,2,1,0:T(8,128)S(1)} %bitcast.3) | data formatting | bytes 1048576
  43.7 0.6 %copy.10 = f32[1,512]{1,0:T(1,128)} copy(f32[1,512]{1,0:T(1,128)S(1)} %get-tuple-element.9) | data formatting | bytes 4096

commit v6 on v5

--- a/solution.py
+++ b/solution.py
@@ -417,8 +417,8 @@
         return goes
 
     def for_each_straight(act):
-        for dy in (2, 1, y_count - 1, 0):
-            for at in range(MID if dy == 0 else DIRECT):
+        for at in range(MID):
+            for dy in (2, 1, y_count - 1, 0) if at < DIRECT else (0,):
                 goes = straight_goes(dy, at)
                 if goes is None:
                     act(straight_copy(dy, at))

time: 44.5 us -> 44.5 us (level)
  no operation moved by 1% of the time
where the time goes in v6:
time: 44.5 us; the launch traced here: 44.3 us
  Pallas kernels  42.2 us (95%)
  local copies, waits for them, and re-layouts  1.37 us (3%)
  between operations  0.64 us (1%)
    pallas_call x1, Pallas kernels, on_device(): pl.pallas_call(functools.partial(kernel, rows, y_count, z_count), out_sha...  42.2 us
    unnamed x2, local copies, waits for them, and re-layouts  1.37 us

profile of v6, /device:TPU:1, one launch (start us, length us, event | category | flops | bytes accessed | tf_op | source)
XLA Modules:
  0.0 44.3 jit_solution(5443225385304041849)
XLA Ops:
  0.6 42.2 %shard_map.68 = (f32[4,32,1024]{2,1,0:T(8,128)S(1)}, f32[1,512]{1,0:T(1,128)S(1)}) custom-call(s32[1,6]{1,0:T(1,128)} %neighbour_hbm.1, s32[1,8]{1,0:T(1,128)} %source_hbm.1, f32[3]{0:T(128)} %force_hbm.1, f32[4,32,1024]{2,1,0:T(8,128)} %bitcast.4, s32[32,1024]{1,0:T(8,128)} %bitcast.5), custom_call_target="tpu_custom_call" | custom-call | tf_op jit(solution)/shard_map/pallas_call | solution.py:565
  42.9 0.8 %copy.9 = f32[1,4,32,1024]{3,2,1,0:T(8,128)} copy(f32[1,4,32,1024]{3,2,1,0:T(8,128)S(1)} %bitcast.3) | data formatting | bytes 1048576
  43.7 0.6 %copy.10 = f32[1,512]{1,0:T(1,128)} copy(f32[1,512]{1,0:T(1,128)S(1)} %get-tuple-element.9) | data formatting | bytes 4096
